TPU v7x, 32 devices: a whole 2x2x4 slice. The times are simulated.
32 devices in a mesh: dp: 16 (over z, y, core), tp: 2 (over x).
Axes of the slice: x: 2, y: 2, z: 4, core: 2. Of those that a mesh axis runs over, the one named last changes fastest.
Arguments:
- x_in: bfloat16 [128, 512, 512], P('dp', 'tp'), may hold values from -6 to 6
- conv_w: bfloat16 [2, 512, 9, 512], P(None, 'tp'), may hold values from -0.09375 to 0.09375
- conv_b: bfloat16 [2, 512], P(None, 'tp'), may hold values from -3 to 3
- ln_gain: bfloat16 [2, 2, 512], P(None, None, 'tp'), may hold values from 0.099609375 to 1.8984375
- ln_bias: bfloat16 [2, 2, 512], P(None, None, 'tp'), may hold values from -2 to 2
- up_w: bfloat16 [2, 512, 512], P(None, None, 'tp'), may hold values from -0.25 to 0.25
- up_b: bfloat16 [2, 512], P(None, 'tp'), may hold values from -3 to 3
- down_w: bfloat16 [2, 512, 512], P(None, 'tp'), may hold values from -0.25 to 0.25
- down_b: bfloat16 [2, 512], P(None, 'tp'), may hold values from -3 to 3
- readout: bfloat16 [512, 6], P('tp'), may hold values from -0.25 to 0.25
- cotangent: bfloat16 [128, 512, 512], P('dp', 'tp'), may hold values from -6 to 6
- masked: int32 [128, 512], P('dp'), may hold values from 0 to 1, as said below
- species: int32 [128], P('dp'), may hold values from 0 to 7
Outputs:
- y_out: bfloat16 [128, 512, 512], P('dp', 'tp')
- grad_x: float32 [128, 512, 512], P('dp', 'tp')
- grad_conv_w: float32 [2, 512, 9, 512], P(None, 'tp')
- grad_conv_b: float32 [2, 512], P(None, 'tp')
- grad_ln_gain: float32 [2, 2, 512], P(None, None, 'tp')
- grad_ln_bias: float32 [2, 2, 512], P(None, None, 'tp')
- grad_up_w: float32 [2, 512, 512], P(None, None, 'tp')
- grad_up_b: float32 [2, 512], P(None, 'tp')
- grad_down_w: float32 [2, 512, 512], P(None, 'tp')
- grad_down_b: float32 [2, 512], P(None, 'tp')
- species_sum: float32 [8, 6], replicated
Inputs may be any that keep to these rules, and one draw needn't show every extreme that they name: In each window, from 25 to 256 positions are masked; the share differs from window to window.
All inputs are finite; a program needn't handle non-finite values.
Results may differ from a plain program's by a relative error of at most 0.02.
Values may be sent and summed in bfloat16 or wider, within the bound.
No kernel may reach another device: no remote copies, remote signals or barrier semaphores. Data moves between devices by JAX's collectives and lax.ppermute only.
A program may use at most 256 MiB of HBM per device.

v0:
```python
import jax
import jax.numpy as jnp
from jax import lax
from jax.sharding import PartitionSpec as P

D = 512
DILATION_FIRST = 2
DILATION_SECOND = 32
SPECIES = 8


EPS = 1e-05


def gelu_slope(tensor):
    normal_cdf = 0.5 * (1.0 + lax.erf(tensor * 0.7071067811865476))
    return normal_cdf + tensor * jnp.exp(-0.5 * tensor * tensor) * 0.3989422804014327


def conv_apply(inputs, weight, dilation):
    length = inputs.shape[1]
    margin = weight.shape[1] // 2 * dilation
    padded = jnp.pad(inputs, ((0, 0), (margin, margin), (0, 0)))
    summed = None
    for offset_tap in range(weight.shape[1]):
        window_part = padded[:, offset_tap * dilation : offset_tap * dilation + length]
        product = jnp.einsum(
            "wld,de->wle", window_part, weight[:, offset_tap], preferred_element_type=jnp.float32
        )
        summed = product if summed is None else summed + product
    return summed


def conv_grads(inputs, grad_low, weight, dilation):
    length = inputs.shape[1]
    half = weight.shape[1] // 2
    margin = half * dilation
    padded = jnp.pad(inputs, ((0, 0), (margin, margin), (0, 0)))
    grad_pad = jnp.pad(grad_low, ((0, 0), (margin, margin), (0, 0)))
    summed = None
    pieces = []
    for offset_tap in range(weight.shape[1]):
        begin = (2 * half - offset_tap) * dilation
        product = jnp.einsum(
            "wle,de->wld",
            grad_pad[:, begin : begin + length],
            weight[:, offset_tap],
            preferred_element_type=jnp.float32,
        )
        summed = product if summed is None else summed + product
        window_part = padded[:, offset_tap * dilation : offset_tap * dilation + length]
        pieces.append(
            jnp.einsum("wld,wle->ed", window_part, grad_low, preferred_element_type=jnp.float32)
        )
    return (summed, jnp.stack(pieces, axis=1))


def normalize(tensor, row_totals):
    sums_row, sums_square = row_totals(jnp.sum(tensor, axis=2), jnp.sum(tensor * tensor, axis=2))
    row_mean = sums_row / D
    row_var = sums_square / D - row_mean * row_mean
    inv_std = lax.rsqrt(row_var + EPS)
    return ((tensor - row_mean[..., None]) * inv_std[..., None], inv_std)


def norm_back(gradient, normed, inv_std, gain, grad_totals):
    scaled = gradient * gain
    sums_row, sums_cross = grad_totals(jnp.sum(scaled, axis=2), jnp.sum(scaled * normed, axis=2))
    return inv_std[..., None] * (
        scaled - (sums_row / D)[..., None] - normed * (sums_cross / D)[..., None]
    )


def layer_forward(hidden, weights, dilation, comms):
    conv_w, conv_b, gains, biases, up_w, up_b, down_w, down_b = weights
    gather_rows, row_totals, down_sum = comms
    act_full = gather_rows(hidden.astype(jnp.bfloat16))
    conv_out = conv_apply(act_full, conv_w, dilation) + conv_b
    first_norm, first_inv = normalize(jax.nn.gelu(conv_out, approximate=False), row_totals)
    middle = hidden + first_norm * gains[0] + biases[0]
    mid_full = gather_rows(middle.astype(jnp.bfloat16))
    up_out = jnp.einsum("wld,df->wlf", mid_full, up_w, preferred_element_type=jnp.float32) + up_b
    inner_act = jax.nn.gelu(up_out, approximate=False).astype(jnp.bfloat16)
    down_out = (
        down_sum(jnp.einsum("wlf,fe->wle", inner_act, down_w, preferred_element_type=jnp.float32))
        + down_b
    )
    second_norm, second_inv = normalize(jax.nn.gelu(down_out, approximate=False), row_totals)
    result = middle + second_norm * gains[1] + biases[1]
    cached = (
        act_full,
        conv_out,
        first_norm,
        first_inv,
        mid_full,
        up_out,
        inner_act,
        down_out,
        second_norm,
        second_inv,
    )
    return (result, cached)


def layer_backward(gradient, cached, weights, dilation, comms_back):
    conv_w, conv_b, gains, biases, up_w, up_b, down_w, down_b = weights
    (
        act_full,
        conv_out,
        first_norm,
        first_inv,
        mid_full,
        up_out,
        inner_act,
        down_out,
        second_norm,
        second_inv,
    ) = cached
    gather_grad, grad_totals, input_sum = comms_back
    gain_second = jnp.sum(gradient * second_norm, axis=(0, 1))
    bias_second = jnp.sum(gradient, axis=(0, 1))
    grad_down = norm_back(gradient, second_norm, second_inv, gains[1], grad_totals) * gelu_slope(
        down_out
    )
    grad_down_b = jnp.sum(grad_down, axis=(0, 1))
    down_full = gather_grad(grad_down.astype(jnp.bfloat16))
    grad_inner = jnp.einsum("wle,fe->wlf", down_full, down_w, preferred_element_type=jnp.float32)
    grad_down_w = jnp.einsum(
        "wlf,wle->fe", inner_act, down_full, preferred_element_type=jnp.float32
    )
    grad_up = grad_inner * gelu_slope(up_out)
    grad_up_b = jnp.sum(grad_up, axis=(0, 1))
    up_low = grad_up.astype(jnp.bfloat16)
    grad_up_w = jnp.einsum("wld,wlf->df", mid_full, up_low, preferred_element_type=jnp.float32)
    grad_mid = gradient + input_sum(
        jnp.einsum("wlf,df->wld", up_low, up_w, preferred_element_type=jnp.float32)
    )
    gain_first = jnp.sum(grad_mid * first_norm, axis=(0, 1))
    bias_first = jnp.sum(grad_mid, axis=(0, 1))
    grad_conv = norm_back(grad_mid, first_norm, first_inv, gains[0], grad_totals) * gelu_slope(
        conv_out
    )
    grad_conv_b = jnp.sum(grad_conv, axis=(0, 1))
    back_part, grad_conv_w = conv_grads(act_full, grad_conv.astype(jnp.bfloat16), conv_w, dilation)
    grad_in = grad_mid + input_sum(back_part)
    collected = (
        grad_conv_w,
        grad_conv_b,
        jnp.stack([gain_first, gain_second]),
        jnp.stack([bias_first, bias_second]),
        grad_up_w,
        grad_up_b,
        grad_down_w,
        grad_down_b,
    )
    return (grad_in, collected)


def species_part(out_low, read_full, rows_mask, rows_species, logit_total):
    logits = logit_total(
        jnp.einsum("wld,dj->wlj", out_low, read_full, preferred_element_type=jnp.float32)
    )
    chances = jax.nn.softmax(logits, axis=-1)
    per_window = jnp.sum(chances * rows_mask[..., None].astype(jnp.float32), axis=1)
    one_hot_bases = (rows_species[None, :] == jnp.arange(SPECIES, dtype=jnp.int32)[:, None]).astype(
        jnp.float32
    )
    return jnp.dot(one_hot_bases, per_window, precision=lax.Precision.HIGHEST) / out_low.shape[1]


def body(
    x_in,
    conv_w,
    conv_b,
    ln_gain,
    ln_bias,
    up_w,
    up_b,
    down_w,
    down_b,
    readout,
    cotangent,
    masked,
    species,
):
    dilation_list = (DILATION_FIRST, DILATION_SECOND)
    depth = conv_w.shape[0]

    def gather_rows(tensor):
        return lax.all_gather(tensor, "tp", axis=2, tiled=True)

    def row_totals(sums_row, sums_square):
        return lax.psum((sums_row, sums_square), "tp")

    def down_sum(tensor):
        return lax.psum_scatter(tensor, "tp", scatter_dimension=2, tiled=True)

    def gather_grad(tensor):
        return lax.all_gather(tensor, "tp", axis=2, tiled=True)

    def grad_totals(sums_row, sums_cross):
        return (
            lax.psum(sums_row.astype(jnp.bfloat16), "tp").astype(jnp.float32),
            lax.psum(sums_cross.astype(jnp.bfloat16), "tp").astype(jnp.float32),
        )

    def input_sum(tensor):
        return lax.psum_scatter(tensor, "tp", scatter_dimension=2, tiled=True)

    def logit_total(tensor):
        return lax.psum(tensor.astype(jnp.bfloat16), "tp").astype(jnp.float32)

    params = (
        jnp.transpose(conv_w, (0, 3, 2, 1)),
        conv_b,
        ln_gain,
        ln_bias,
        up_w,
        up_b,
        down_w,
        down_b,
    )
    hidden = jnp.swapaxes(x_in, 1, 2).astype(jnp.float32)
    grad_top = jnp.swapaxes(cotangent, 1, 2).astype(jnp.float32)
    comms = (gather_rows, row_totals, down_sum)
    comms_back = (gather_grad, grad_totals, input_sum)
    stored = []
    for block_index in range(depth):
        weights = tuple((member[block_index] for member in params))
        hidden, cached = layer_forward(hidden, weights, dilation_list[block_index], comms)
        stored.append(cached)
    out_low = hidden.astype(jnp.bfloat16)
    species_local = species_part(out_low, readout, masked, species, logit_total)
    gradient = grad_top
    results = [None] * depth
    for block_index in reversed(range(depth)):
        weights = tuple((member[block_index] for member in params))
        gradient, results[block_index] = layer_backward(
            gradient, stored[block_index], weights, dilation_list[block_index], comms_back
        )
    stacked_tensor = tuple((jnp.stack([entry[slot] for entry in results]) for slot in range(8)))
    out_block = jnp.swapaxes(out_low, 1, 2)
    grad_block = jnp.swapaxes(gradient, 1, 2)
    totals = (
        lax.psum(stacked_tensor[0].astype(jnp.bfloat16), "dp").astype(jnp.float32),
        lax.psum(stacked_tensor[1].astype(jnp.bfloat16), "dp").astype(jnp.float32),
        lax.psum(stacked_tensor[2].astype(jnp.bfloat16), "dp").astype(jnp.float32),
        lax.psum(stacked_tensor[3].astype(jnp.bfloat16), "dp").astype(jnp.float32),
        lax.psum(stacked_tensor[4].astype(jnp.bfloat16), "dp").astype(jnp.float32),
        lax.psum(stacked_tensor[5].astype(jnp.bfloat16), "dp").astype(jnp.float32),
        lax.psum(stacked_tensor[6].astype(jnp.bfloat16), "dp").astype(jnp.float32),
        lax.psum(stacked_tensor[7].astype(jnp.bfloat16), "dp").astype(jnp.float32),
        lax.psum(species_local.astype(jnp.bfloat16), "dp").astype(jnp.float32),
    )
    return (
        out_block,
        grad_block,
        totals[0],
        totals[1],
        totals[2],
        totals[3],
        totals[4],
        totals[5],
        totals[6],
        totals[7],
        totals[8],
    )


def solution(mesh):
    placed = (
        P("dp", "tp", None),
        P(None, "tp", None, None),
        P(None, "tp"),
        P(None, None, "tp"),
        P(None, None, "tp"),
        P(None, None, "tp"),
        P(None, "tp"),
        P(None, "tp", None),
        P(None, "tp"),
        P("tp", None),
        P("dp", "tp", None),
        P("dp", None),
        P("dp"),
    )
    return jax.shard_map(
        body,
        mesh=mesh,
        in_specs=placed,
        out_specs=(
            P("dp", "tp", None),
            P("dp", "tp", None),
            P(None, "tp", None, None),
            P(None, "tp"),
            P(None, None, "tp"),
            P(None, None, "tp"),
            P(None, None, "tp"),
            P(None, "tp"),
            P(None, "tp", None),
            P(None, "tp"),
            P(),
        ),
        check_vma=False,
    )
```

profile of v0, /device:TPU:0, one launch (start us, length us, event | category | flops | bytes accessed | tf_op | source)
XLA Modules:
  0.0 1583.2 jit_solution(10781209324136519478)
XLA Ops:
  11.3 6.6 copy.25
  22.3 48.4 %all-gather.7.cloned.1.call-done = bf16[8,512,512]{2,1,0:T(8,128)(2,1)} async-done(((bf16[8,512,256]{2,1,0:T(8,128)(2,1)}), bf16[8,512,512]{2,1,0:T(8,128)(2,1)}) %all-gather.7.cloned.1.call-update) | async-done | bytes 4194320 | tf_op jit(solution)/shard_map/all_gather | solution.py:190
  70.7 5.6 fusion.91
  98.9 14.8 fusion.311
  113.7 12.4 fusion.403
  126.1 7.2 all-reduce.7
  137.4 57.9 %all-gather.9.cloned.1.call-done = bf16[8,512,512]{2,1,0:T(8,128)(2,1)} async-done(((bf16[8,512,256]{2,1,0:T(8,128)(2,1)}), bf16[8,512,512]{2,1,0:T(8,128)(2,1)}) %all-gather.9.cloned.1.call-update) | async-done | bytes 4194320 | tf_op jit(solution)/shard_map/all_gather | solution.py:190
  201.5 9.5 fusion.4
  217.7 98.7 %reduce-scatter.7.cloned.1.call-done = f32[8,512,256]{2,1,0:T(8,128)} async-done(((f32[8,512,512]{2,1,0:T(8,128)}), f32[8,512,256]{2,1,0:T(8,128)}) %reduce-scatter.7.cloned.1.call-update) | async-done | bytes 4194320 | tf_op jit(solution)/shard_map/reduce_scatter | solution.py:196
  316.4 22.1 %fusion.402 = (f32[8,512]{1,0:T(8,128)S(1)}, f32[8,512]{1,0:T(8,128)S(1)}, f32[8,512,256]{2,1,0:T(8,128)}) fusion(f32[8,512,256]{2,1,0:T(8,128)} %reduce-scatter.7.cloned.1.call-done, f32[256]{0:T(256)S(1)} %bitcast.513), kind=kLoop, calls=%fused_computation.525 | loop fusion | flops 71294976 | bytes 8422400 | tf_op jit(solution)/shard_map/reduce_sum | solution.py:59
  338.5 7.2 all-reduce.6
  345.7 8.8 fusion.414
  354.5 58.0 %all-gather.11.cloned.1.call-done = bf16[8,512,512]{2,1,0:T(8,128)(2,1)} async-done(((bf16[8,512,256]{2,1,0:T(8,128)(2,1)}), bf16[8,512,512]{2,1,0:T(8,128)(2,1)}) %all-gather.11.cloned.1.call-update) | async-done | bytes 4194320 | tf_op jit(solution)/shard_map/all_gather | solution.py:190
  440.4 12.3 fusion.312
  452.7 11.1 fusion.401
  463.8 7.2 all-reduce.5
  476.2 58.0 %all-gather.13.cloned.1.call-done = bf16[8,512,512]{2,1,0:T(8,128)(2,1)} async-done(((bf16[8,512,256]{2,1,0:T(8,128)(2,1)}), bf16[8,512,512]{2,1,0:T(8,128)(2,1)}) %all-gather.13.cloned.1.call-update) | async-done | bytes 4194320 | tf_op jit(solution)/shard_map/all_gather | solution.py:190
  540.3 9.5 fusion.11
  559.2 96.0 %reduce-scatter.9.cloned.1.call-done = f32[8,512,256]{2,1,0:T(8,128)} async-done(((f32[8,512,512]{2,1,0:T(8,128)}), f32[8,512,256]{2,1,0:T(8,128)}) %reduce-scatter.9.cloned.1.call-update) | async-done | bytes 4194320 | tf_op jit(solution)/shard_map/reduce_scatter | solution.py:196
  655.2 12.7 fusion.400
  667.8 7.2 all-reduce.4
  679.6 8.3 all-reduce.13
  687.9 8.9 fusion.406
  696.8 56.8 %all-gather.15.cloned.1.call-done = bf16[8,512,512]{2,1,0:T(8,128)(2,1)} async-done(((bf16[8,512,256]{2,1,0:T(8,128)(2,1)}), bf16[8,512,512]{2,1,0:T(8,128)(2,1)}) %all-gather.15.cloned.1.call-update) | async-done | bytes 4194320 | tf_op jit(solution)/shard_map/all_gather | solution.py:199
  753.7 5.9 fusion.417
  765.7 99.4 %reduce-scatter.11.cloned.1.call-done = f32[8,512,256]{2,1,0:T(8,128)} async-done(((f32[8,512,512]{2,1,0:T(8,128)}), f32[8,512,256]{2,1,0:T(8,128)}) %reduce-scatter.11.cloned.1.call-update) | async-done | bytes 4194320 | tf_op jit(solution)/shard_map/reduce_scatter | solution.py:208
  865.0 7.0 multiply_reduce_fusion
  872.0 6.9 all-reduce.12
  878.9 10.5 fusion.410
  925.6 25.7 %add_add_fusion.1 = f32[8,512,512]{2,1,0:T(8,128)} fusion(f32[8,512,512]{2,1,0:T(8,128)} %fusion.145, f32[8,512,512]{2,1,0:T(8,128)} %fusion.144, f32[8,512,512]{2,1,0:T(8,128)} %fusion.143, f32[8,512,512]{2,1,0:T(8,128)} %fusion.340, f32[8,512,512]{2,1,0:T(8,128)} %fusion.142, f32[8,512,512]{2,1,0:T(8,128)} %fusion.141, f32[8,512,512]{2,1,0:T(8,128)} %fusion.139, ...), kind=kOutput, calls=%fused_computation.9 | convolution fusion | flops 1090519040 | bytes 77856768 | tf_op jit(solution)/shard_map/wle,de->wld/dot_general | solution.py:44
  951.3 100.5 %reduce-scatter.13.cloned.1.call-done = f32[8,512,256]{2,1,0:T(8,128)} async-done(((f32[8,512,512]{2,1,0:T(8,128)}), f32[8,512,256]{2,1,0:T(8,128)}) %reduce-scatter.13.cloned.1.call-update) | async-done | bytes 4194320 | tf_op jit(solution)/shard_map/reduce_scatter | solution.py:208
  1051.8 7.4 multiply_reduce_fusion.1
  1059.2 6.9 all-reduce.11
  1066.2 9.1 fusion.404
  1075.3 57.9 %all-gather.17.cloned.1.call-done = bf16[8,512,512]{2,1,0:T(8,128)(2,1)} async-done(((bf16[8,512,256]{2,1,0:T(8,128)(2,1)}), bf16[8,512,512]{2,1,0:T(8,128)(2,1)}) %all-gather.17.cloned.1.call-update) | async-done | bytes 4194320 | tf_op jit(solution)/shard_map/all_gather | solution.py:199
  1133.2 5.4 fusion.418
  1171.6 72.6 %reduce-scatter.15.cloned.1.call-done = f32[8,512,256]{2,1,0:T(8,128)} async-done(((f32[8,512,512]{2,1,0:T(8,128)}), f32[8,512,256]{2,1,0:T(8,128)}) %reduce-scatter.15.cloned.1.call-update) | async-done | bytes 4194320 | tf_op jit(solution)/shard_map/reduce_scatter | solution.py:208
  1244.2 8.0 multiply_reduce_fusion.2
  1253.2 20.3 %all-reduce.19.cloned.1.call-done = (bf16[8,512]{1,0:T(8,128)(2,1)}, bf16[8,512]{1,0:T(8,128)(2,1)}, bf16[8,512,6]{1,2,0:T(8,128)(2,1)}) async-done(((bf16[8,512]{1,0:T(8,128)(2,1)}, bf16[8,512]{1,0:T(8,128)(2,1)}, bf16[8,512,6]{1,2,0:T(8,128)(2,1)}), (bf16[8,512]{1,0:T(8,128)(2,1)}, bf16[8,512]{1,0:T(8,128)(2,1)}, bf16[8,512,6]{1,2,0:T(8,128)(2,1)})) %all-reduce.19.cloned.1.call-update) | async-done | bytes 65552 | tf_op jit(solution)/shard_map/psum | solution.py:204
  1274.9 8.1 fusion.408
  1329.7 5.4 fusion.157
  1335.1 26.2 %add_add_fusion = f32[8,512,512]{2,1,0:T(8,128)} fusion(f32[8,512,512]{2,1,0:T(8,128)} %fusion.147, f32[8,512,512]{2,1,0:T(8,128)} %fusion.149, f32[8,512,512]{2,1,0:T(8,128)} %fusion.151, f32[8,512,512]{2,1,0:T(8,128)} %fusion.338, f32[8,512,512]{2,1,0:T(8,128)} %fusion.153, f32[8,512,512]{2,1,0:T(8,128)} %fusion.155, f32[8,512,512]{2,1,0:T(8,128)} %fusion.159, ...), kind=kOutput, calls=%fused_computation.8 | convolution fusion | flops 1090519040 | bytes 77856768 | tf_op jit(solution)/shard_map/wle,de->wld/dot_general | solution.py:44
  1366.8 34.6 %all-reduce.8 = (bf16[2,256]{1,0:T(2,128)(2,1)S(1)}, bf16[2,2,256]{2,1,0:T(2,128)(2,1)S(1)}, bf16[2,2,256]{2,1,0:T(2,128)(2,1)S(1)}, bf16[2,256]{1,0:T(2,128)(2,...) all-reduce(bf16[2,256]{1,0:T(2,128)(2,1)S(1)} %pad_maximum_fusion.5, ...), channel_id=1, replica_groups=mesh['dp'=16,'tp'=2] {'dp'}, use_global_device_ids=true, to_apply=%region_41.42 | all-reduce | flops 3632 | bytes 14528 | tf_op jit(solution)/shard_map/psum | solution.py:246
  1404.9 58.6 %all-reduce.17.cloned.1.call-done = (bf16[2,256,9,512]{3,1,2,0:T(8,128)(2,1)}, bf16[2,512,256]{2,1,0:T(8,128)(2,1)}, bf16[2,256,512]{2,1,0:T(8,128)(2,1)}) async-done(((bf16[2,256,9,512]{3,1,2,0:T(8,128)(2,1)}, bf16[2,512,256]{2,1,0:T(8,128)(2,1)}, bf16[2,256,512]{2,1,0:T(8,128)(2,1)}), (bf16[2,256,9,512]{3,1,2,0:T(8,128)(2,1)}, bf16[2,512,256]{2,1,0:T(8,128)(2,1)}, ...) | async-done | bytes 5767184 | tf_op jit(solution)/shard_map/psum | solution.py:245
  1467.7 7.4 convert_element_type.276
  1475.1 89.9 %reduce-scatter.17.cloned.1.call-done = f32[8,512,256]{2,1,0:T(8,128)} async-done(((f32[8,512,512]{2,1,0:T(8,128)}), f32[8,512,256]{2,1,0:T(8,128)}) %reduce-scatter.17.cloned.1.call-update) | async-done | bytes 4194320 | tf_op jit(solution)/shard_map/reduce_scatter | solution.py:208
  1565.0 6.0 add_bitcast_fusion
  1570.9 5.3 copy.68
  (255 shorter events, 238.0 us)
Async XLA Ops:
  7.2 1143.9 %copy-start = (bf16[256,6]{0,1:T(8,128)(2,1)S(1)}, bf16[256,6]{0,1:T(8,128)(2,1)}, u32[]{:S(2)}) copy-start(bf16[256,6]{0,1:T(8,128)(2,1)} %param.22) | copy-start | bytes 9220
  7.2 63.5 %all-gather.7.cloned.1.call-start = ((), (), s32[]{:S(2)}) async-start(), calls=%async_computation.6 | async-start | bytes 6291456 | tf_op jit(solution)/shard_map/all_gather | solution.py:190
  11.2 6.7 copy-start.40
  11.2 6.7 copy-start.38
  11.2 6.7 copy-start.39
  11.2 184.2 %all-gather.9.cloned.1.call-start = ((), (), s32[]{:S(2)}) async-start(), calls=%async_computation.7 | async-start | bytes 6291456 | tf_op jit(solution)/shard_map/all_gather | solution.py:190
  17.9 327.7 %copy-start.35 = (f32[1,1,256]{2,1,0:T(1,128)}, f32[1,1,256]{2,1,0:T(1,128)S(1)}, u32[]{:S(2)}) copy-start(f32[1,1,256]{2,1,0:T(1,128)S(1)} %get-tuple-element.105) | copy-start | bytes 3076
  22.3 76.6 %copy-start.10 = (bf16[512,9,256]{2,0,1:T(8,128)(2,1)}, bf16[512,9,256]{2,0,1:T(8,128)(2,1)S(1)}, u32[]{:S(2)}) copy-start(bf16[512,9,256]{2,0,1:T(8,128)(2,1)S(1)} %get-tuple-element.93) | copy-start | bytes 7077892
  70.7 5.6 copy-start.1
  113.7 19.6 %copy-start.6 = (bf16[8,256,512]{1,2,0:T(8,128)(2,1)S(1)}, bf16[8,256,512]{1,2,0:T(8,128)(2,1)}, u32[]{:S(2)}) copy-start(bf16[8,256,512]{1,2,0:T(8,128)(2,1)} %copy.24) | copy-start | bytes 6291460
  133.3 212.4 %copy-start.31 = (f32[8,512]{1,0:T(8,128)}, f32[8,512]{1,0:T(8,128)S(1)}, u32[]{:S(2)}) copy-start(f32[8,512]{1,0:T(8,128)S(1)} %get-tuple-element.101) | copy-start | bytes 49156
  133.3 212.4 %copy-start.33 = (f32[8,512]{1,0:T(8,128)}, f32[8,512]{1,0:T(8,128)S(1)}, u32[]{:S(2)}) copy-start(f32[8,512]{1,0:T(8,128)S(1)} %get-tuple-element.102) | copy-start | bytes 49156
  133.4 4.0 copy-start.41
  133.4 62.0 %copy-start.29 = (bf16[2,512,256]{2,1,0:T(8,128)(2,1)S(1)}, bf16[2,512,256]{2,1,0:T(8,128)(2,1)}, u32[]{:S(2)}) copy-start(bf16[2,512,256]{2,1,0:T(8,128)(2,1)} %param.18) | copy-start | bytes 1572868
  137.4 179.0 %reduce-scatter.7.cloned.1.call-start = ((), (), s32[]{:S(2)}) async-start(), calls=%async_computation.8 | async-start | bytes 12582912 | tf_op jit(solution)/shard_map/reduce_scatter | solution.py:196
  137.4 62.2 %copy-start.43 = (f32[1,256]{1,0:T(1,128)}, f32[1,256]{1,0:T(1,128)S(1)}, u32[]{:S(2)}) copy-start(f32[1,256]{1,0:T(1,128)S(1)} %get-tuple-element.114) | copy-start | bytes 3076
  199.6 12.7 copy-start.28
  217.0 195.5 %all-gather.11.cloned.1.call-start = ((), (), s32[]{:S(2)}) async-start(), calls=%async_computation.9 | async-start | bytes 6291456 | tf_op jit(solution)/shard_map/all_gather | solution.py:190
  354.5 179.7 %all-gather.13.cloned.1.call-start = ((), (), s32[]{:S(2)}) async-start(), calls=%async_computation.10 | async-start | bytes 6291456 | tf_op jit(solution)/shard_map/all_gather | solution.py:190
  412.5 5.3 copy-start.3
  412.5 5.3 copy-start.12
  452.7 11.1 copy-start.5
  471.0 63.2 %copy-start.30 = (bf16[2,512,256]{2,1,0:T(8,128)(2,1)S(1)}, bf16[2,512,256]{2,1,0:T(8,128)(2,1)}, u32[]{:S(2)}) copy-start(bf16[2,512,256]{2,1,0:T(8,128)(2,1)} %param.18) | copy-start | bytes 1572868
  476.1 179.0 %reduce-scatter.9.cloned.1.call-start = ((), (), s32[]{:S(2)}) async-start(), calls=%async_computation.11 | async-start | bytes 12582912 | tf_op jit(solution)/shard_map/reduce_scatter | solution.py:196
  555.8 197.9 %all-gather.15.cloned.1.call-start = ((), (), s32[]{:S(2)}) async-start(), calls=%async_computation.12 | async-start | bytes 6291456 | tf_op jit(solution)/shard_map/all_gather | solution.py:199
  696.8 168.2 %reduce-scatter.11.cloned.1.call-start = ((), (), s32[]{:S(2)}) async-start(), calls=%async_computation.13 | async-start | bytes 12582912 | tf_op jit(solution)/shard_map/reduce_scatter | solution.py:208
  765.6 286.2 %reduce-scatter.13.cloned.1.call-start = ((), (), s32[]{:S(2)}) async-start(), calls=%async_computation.14 | async-start | bytes 12582912 | tf_op jit(solution)/shard_map/reduce_scatter | solution.py:208
  878.9 10.5 copy-start.13
  951.3 182.0 %all-gather.17.cloned.1.call-start = ((), (), s32[]{:S(2)}) async-start(), calls=%async_computation.15 | async-start | bytes 6291456 | tf_op jit(solution)/shard_map/all_gather | solution.py:199
  1066.1 67.1 %copy-start.44 = (f32[1,256]{1,0:T(1,128)S(1)}, f32[1,256]{1,0:T(1,128)}, u32[]{:S(2)}) copy-start(f32[1,256]{1,0:T(1,128)} %copy-done.43) | copy-start | bytes 3076
  1075.3 169.0 %reduce-scatter.15.cloned.1.call-start = ((), (), s32[]{:S(2)}) async-start(), calls=%async_computation.16 | async-start | bytes 12582912 | tf_op jit(solution)/shard_map/reduce_scatter | solution.py:208
  1144.7 128.9 %all-reduce.19.cloned.1.call-start = ((), (), s32[]{:S(2)}) async-start(), calls=%async_computation.19 | async-start | bytes 163840 | tf_op jit(solution)/shard_map/psum | solution.py:204
  1145.1 4.3 copy-start.17
  1145.1 4.7 copy-start.21
  1149.8 3.5 copy-start.4
  1163.5 3.0 copy-start.20
  1166.5 2.5 copy-start.8
  1166.5 3.9 copy-start.22
  1170.3 73.9 %copy-start.32 = (f32[8,512]{1,0:T(8,128)S(1)}, f32[8,512]{1,0:T(8,128)}, u32[]{:S(2)}) copy-start(f32[8,512]{1,0:T(8,128)} %copy-done.31) | copy-start | bytes 49156
  1170.3 73.9 %copy-start.34 = (f32[8,512]{1,0:T(8,128)S(1)}, f32[8,512]{1,0:T(8,128)}, u32[]{:S(2)}) copy-start(f32[8,512]{1,0:T(8,128)} %copy-done.33) | copy-start | bytes 49156
  1170.3 73.9 %copy-start.36 = (f32[1,1,256]{2,1,0:T(1,128)S(1)}, f32[1,1,256]{2,1,0:T(1,128)}, u32[]{:S(2)}) copy-start(f32[1,1,256]{2,1,0:T(1,128)} %copy-done.35) | copy-start | bytes 3076
  1252.3 211.2 %all-reduce.17.cloned.1.call-start = ((), (), s32[]{:S(2)}) async-start(), calls=%async_computation.18 | async-start | bytes 11534336 | tf_op jit(solution)/shard_map/psum | solution.py:245
  1274.9 8.1 copy-start.11
  1310.2 4.5 copy-start.2
  1329.6 235.3 %reduce-scatter.17.cloned.1.call-start = ((), (), s32[]{:S(2)}) async-start(), calls=%async_computation.17 | async-start | bytes 12582912 | tf_op jit(solution)/shard_map/reduce_scatter | solution.py:208
  1361.4 2.4 copy-start.15
  1361.5 4.9 copy-start.27
  1361.5 5.2 copy-start.50
  (18 other events, 32.8 us)
Sparse Core Ops, SparseCore 0:
  11.3 59.3 all-gather.6
  137.5 57.8 all-gather.8
  217.1 99.2 reduce-scatter.6
  354.6 57.8 all-gather.10
  476.3 57.8 all-gather.12
  555.9 99.2 reduce-scatter.8
  696.9 56.7 all-gather.14
  765.7 99.2 reduce-scatter.10
  951.4 100.3 reduce-scatter.12
  1075.4 57.8 all-gather.16
  1144.8 99.2 reduce-scatter.14
  1252.4 21.0 all-reduce.18
  1329.7 133.7 all-reduce.16
  1465.7 99.1 reduce-scatter.16
where the time goes:
time: 1590 us; the launch traced here: 1580 us
  waiting for transfers between devices  973 us (61%)
  matrix products  279 us (18%)
  other arithmetic  188 us (12%)
  blocking collectives  85.3 us (5%)
  local copies, waits for them, and re-layouts  41.1 us (3%)
    reduce_scatter x4, waiting for transfers between devices, input_sum(): return lax.psum_scatter(tensor, 'tp', scatter_dimension=2, tiled=True)  362 us
    all_gather x4, waiting for transfers between devices, gather_rows(): return lax.all_gather(tensor, 'tp', axis=2, tiled=True)  222 us
    reduce_scatter x2, waiting for transfers between devices, down_sum(): return lax.psum_scatter(tensor, 'tp', scatter_dimension=2, tiled=True)  195 us
    dot_general x18, matrix products, conv_grads(): jnp.einsum('wle,de->wld', grad_pad[:, begin:begin + length], weight[:, of...  125 us
    all_gather x2, waiting for transfers between devices, gather_grad(): return lax.all_gather(tensor, 'tp', axis=2, tiled=True)  115 us
    dot_general x18, matrix products, conv_apply(): jnp.einsum('wld,de->wle', window_part, weight[:, offset_tap], preferred_e...  83.2 us
    psum x1, waiting for transfers between devices, body(): lax.psum(stacked_tensor[0].astype(jnp.bfloat16), 'dp').astype(jnp.float32)  58.6 us
    reduce_sum x4, other arithmetic, normalize(): jnp.sum(tensor, axis=2)  58.2 us
  transfers between devices with their start and end apart: 14, of which 14 were waited for; matrix products, arithmetic and copies ran while one was open for 6% of the time, Pallas kernels for 0%

commit v1 on v0

v1 whole, which is shorter than its diff:
```python
import functools

import jax
import jax.numpy as jnp
from jax import lax
from jax.experimental import pallas as pl
from jax.experimental.pallas import tpu as pltpu
from jax.sharding import Mesh
from jax.sharding import PartitionSpec as P

DILATIONS = (2, 32)
SPECIES = 8
EPS = 1e-05
BF = jnp.bfloat16
F32 = jnp.float32
DP = ("z", "y", "core")
STEP = 16
VMEM_BYTES = 58 * 2**20
CONV_B, GAIN_A, BIAS_A, UP_B, DOWN_B, GAIN_B, BIAS_B = range(7)
COLUMNS = 8


def shifted(rows, by):
    if by == 0:
        return rows
    blank = jnp.zeros((rows.shape[0], abs(by)), rows.dtype)
    if by > 0:
        return jnp.concatenate([rows[:, by:], blank], axis=1)
    return jnp.concatenate([blank, rows[:, :by]], axis=1)


def fold(tile):
    return sum(tile[at : at + 8] for at in range(0, tile.shape[0], 8))


def fold_lanes(tile):
    return sum(tile[:, at : at + 128] for at in range(0, tile.shape[1], 128))


def gelu_pair(x):
    cdf = 0.5 + 0.5 * lax.erf(x * 0.7071067811865476)
    return x * cdf, cdf + x * jnp.exp(-0.5 * x * x) * 0.3989422804014327


def nn(left, right):
    return jnp.dot(left, right, preferred_element_type=F32)


def tn(left, right):
    return lax.dot_general(left, right, (((0,), (0,)), ((), ())), preferred_element_type=F32)


def nt(left, right):
    return lax.dot_general(left, right, (((1,), (1,)), ((), ())), preferred_element_type=F32)


def steps(size):
    return [slice(at, at + STEP) for at in range(0, size, STEP)]


def place(pieces, me, target):
    ways = len(pieces)
    for back, piece in enumerate(pieces):
        size = piece.shape[1]
        spot = lax.rem(me + (ways - back), ways) * size
        target[pl.ds(pl.multiple_of(spot, size), size), :] = piece[0]


def norm_stats(total, square, width):
    mean = jnp.sum(total, axis=0, keepdims=True) / width
    var = jnp.sum(square, axis=0, keepdims=True) / width - mean * mean
    return mean, lax.rsqrt(var + EPS)


def activate_and_sum(pre, col, pc, slope_ref):
    size, length = pre.shape
    total = jnp.zeros((8, length), F32)
    square = jnp.zeros((8, length), F32)
    for rows in steps(size):
        value, slope = gelu_pair(pre[rows, :] + pc[rows, col : col + 1])
        pre[rows, :] = value
        slope_ref[0, rows, :] = slope.astype(BF)
        total = total + fold(value)
        square = square + fold(value * value)
    return norm_stats(total, square, size)


def forward_kernel(layer, n_in, n_out, taps, *refs):
    me_ref, w, pc = refs[:3]
    pieces = refs[3 : 3 + n_in]
    at = 3 + n_in
    reads = None
    if n_out:
        reads = refs[at : at + 2]
        at += 2
    outs = refs[at : at + 8]
    at += 8
    a_ref, b_ref, n1_ref, s1_ref, su_ref, v_ref, s2_ref, n2_ref = outs
    extra = refs[at : at + n_out + (1 if n_out else 0)]
    at += len(extra)
    act, wide, pre, mid = refs[at:]
    me = me_ref[0]
    size, length = act.shape
    base = layer * COLUMNS
    half = taps // 2
    place(pieces, me, act)
    a_ref[0] = act[...]
    for tap in range(taps):
        wide[tap] = shifted(act[...], (tap - half) * DILATIONS[layer])
    total = nn(w[0], wide[0])
    for tap in range(1, taps):
        total = total + nn(w[tap], wide[tap])
    pre[...] = total
    mean, inv = activate_and_sum(pre, base + CONV_B, pc, s1_ref)
    for rows in steps(size):
        normed = (pre[rows, :] - mean) * inv
        m = (
            act[rows, :].astype(F32)
            + normed * pc[rows, base + GAIN_A : base + GAIN_A + 1]
            + pc[rows, base + BIAS_A : base + BIAS_A + 1]
        )
        n1_ref[0, rows, :] = normed.astype(BF)
        s1_ref[0, rows, :] = (s1_ref[0, rows, :].astype(F32) * inv).astype(BF)
        mid[rows, :] = m
        b_ref[0, rows, :] = m.astype(BF)
    pre[...] = nn(w[taps], b_ref[0])
    for rows in steps(size):
        value, slope = gelu_pair(pre[rows, :] + pc[rows, base + UP_B : base + UP_B + 1])
        v_ref[0, rows, :] = value.astype(BF)
        su_ref[0, rows, :] = slope.astype(BF)
    pre[...] = tn(w[taps + 1], v_ref[0])
    mean, inv = activate_and_sum(pre, base + DOWN_B, pc, s2_ref)
    for rows in steps(size):
        normed = (pre[rows, :] - mean) * inv
        out = (
            mid[rows, :]
            + normed * pc[rows, base + GAIN_B : base + GAIN_B + 1]
            + pc[rows, base + BIAS_B : base + BIAS_B + 1]
        )
        n2_ref[0, rows, :] = normed.astype(BF)
        s2_ref[0, rows, :] = (s2_ref[0, rows, :].astype(F32) * inv).astype(BF)
        act[rows, :] = out.astype(BF)
    if not n_out:
        return
    readout, mask_ref = reads
    chance_ref = extra[n_out]
    part = size // n_out
    for ahead in range(n_out):
        spot = lax.rem(me + ahead, n_out) * part
        extra[ahead][0] = act[pl.ds(pl.multiple_of(spot, part), part), :]
    logits = nn(readout[...], act[...])
    seat = lax.broadcasted_iota(jnp.int32, logits.shape, 0)
    logits = jnp.where(seat < 6, logits, -1e30)
    raised = jnp.exp(logits - jnp.max(logits, axis=0, keepdims=True))
    chance = raised / jnp.sum(raised, axis=0, keepdims=True)
    chance_ref[0] = fold_lanes(chance * mask_ref[0].astype(F32))


def first_kernel(layer, n_in, taps, *refs):
    n_args = 3 + n_in
    outs = refs[n_args : n_args + 9]
    rest = refs[n_args + 9 :]
    forward_kernel(layer, n_in, 0, taps, *refs[:n_args], *outs[:8], *rest)
    outs[8][0] = rest[0][...]


def chain(layer, taps, first, last, grad, kept, w, pc, outs, work):
    b_ref, n1_ref, s1_ref, su_ref, v_ref, s2_ref, n2_ref = kept
    dc_ref, dm_ref, ff_ref, small_ref = outs
    pre, low, ff_sum, row_sums = work
    size, length = pre.shape
    base = layer * COLUMNS

    @pl.when(first)
    def _():
        ff_sum[...] = jnp.zeros_like(ff_sum)
        row_sums[...] = jnp.zeros_like(row_sums)

    def gather_q(gain_col, normed_ref, gain_slot, bias_slot):
        total = jnp.zeros((8, length), F32)
        cross = jnp.zeros((8, length), F32)
        for rows in steps(size):
            g = grad[rows, :]
            normed = normed_ref[0, rows, :].astype(F32)
            product = g * normed
            row_sums[gain_slot, rows, :] += fold_lanes(product)
            row_sums[bias_slot, rows, :] += fold_lanes(g)
            gain = pc[rows, gain_col : gain_col + 1]
            total = total + fold(g * gain)
            cross = cross + fold(product * gain)
        return (
            jnp.sum(total, axis=0, keepdims=True) / size,
            jnp.sum(cross, axis=0, keepdims=True) / size,
        )

    def back(gain_col, normed_ref, slope_ref, bias_slot, target):
        mean_q, mean_qn = gather_q(gain_col, normed_ref, bias_slot + 1, bias_slot + 2)
        for rows in steps(size):
            q = grad[rows, :] * pc[rows, gain_col : gain_col + 1]
            normed = normed_ref[0, rows, :].astype(F32)
            d = slope_ref[0, rows, :].astype(F32) * (q - mean_q - normed * mean_qn)
            row_sums[bias_slot, rows, :] += fold_lanes(d)
            target(rows, d.astype(BF))

    def put_low(rows, value):
        low[rows, :] = value

    def put_dc(rows, value):
        dc_ref[0, rows, :] = value

    back(base + GAIN_B, n2_ref, s2_ref, DOWN_B, put_low)
    pre[...] = nn(w[taps + 1], low[...])
    ff_sum[1] += nt(v_ref[0], low[...])
    for rows in steps(size):
        du = pre[rows, :] * su_ref[0, rows, :].astype(F32)
        row_sums[UP_B, rows, :] += fold_lanes(du)
        low[rows, :] = du.astype(BF)
    pre[...] = tn(w[taps], low[...])
    ff_sum[0] += nt(low[...], b_ref[0])
    for rows in steps(size):
        dm = grad[rows, :] + pre[rows, :]
        grad[rows, :] = dm
        dm_ref[0, rows, :] = dm.astype(BF)
    back(base + GAIN_A, n1_ref, s1_ref, CONV_B, put_dc)

    @pl.when(last)
    def _():
        ff_ref[...] = ff_sum[...].astype(BF)
        for rows in steps(size):
            seat = lax.broadcasted_iota(jnp.int32, (STEP, 128), 1)
            table = jnp.zeros((STEP, 128), F32)
            for slot in range(7):
                column = jnp.sum(row_sums[slot, rows, :], axis=1, keepdims=True)
                table = jnp.where(seat == slot, column, table)
            small_ref[rows, :] = table


def conv_back(layer, taps, dc, dm_ref, w, wide, grad):
    half = taps // 2
    for tap in range(taps):
        wide[tap] = shifted(dc, -(tap - half) * DILATIONS[layer])
    total = tn(w[0], wide[0])
    for tap in range(1, taps):
        total = total + tn(w[tap], wide[tap])
    grad[...] = total
    for rows in steps(grad.shape[0]):
        grad[rows, :] = grad[rows, :] + dm_ref[0, rows, :].astype(F32)


def top_kernel(layer, n_in, taps, *refs):
    me_ref, w, pc = refs[:3]
    pieces = refs[3 : 3 + n_in]
    kept = refs[3 + n_in : 10 + n_in]
    outs = refs[10 + n_in : 14 + n_in]
    grad, *work = refs[14 + n_in :]
    me = me_ref[0]
    ways = n_in
    for back, piece in enumerate(pieces):
        part = piece.shape[1]
        spot = pl.multiple_of(lax.rem(me + (ways - back), ways) * part, part)
        grad[pl.ds(spot, part), :] = piece[0].astype(F32)
    here = pl.program_id(0)
    chain(layer, taps, here == 0, here == pl.num_programs(0) - 1, grad, kept, w, pc, outs, work)


def middle_kernel(layer, taps, *refs):
    above_w, w, pc, dc_in, dm_in = refs[:5]
    kept = refs[5:12]
    outs = refs[12:16]
    grad, wide, *work = refs[16:]
    conv_back(layer + 1, taps, dc_in[0], dm_in, above_w, wide, grad)
    here = pl.program_id(0)
    chain(layer, taps, here == 0, here == pl.num_programs(0) - 1, grad, kept, w, pc, outs, work)


def bottom_kernel(layer, taps, n_out, *refs):
    me_ref, w, dc_in, dm_in = refs[:4]
    own_ref = refs[4]
    others = refs[5 : 4 + n_out]
    grad, wide = refs[4 + n_out :]
    conv_back(layer, taps, dc_in[0], dm_in, w, wide, grad)
    me = me_ref[0]
    part = own_ref.shape[1]
    own_ref[0] = grad[pl.ds(pl.multiple_of(me * part, part), part), :]
    for ahead, ref in enumerate(others, start=1):
        spot = pl.multiple_of(lax.rem(me + ahead, n_out) * part, part)
        ref[0] = grad[pl.ds(spot, part), :].astype(BF)


def weight_kernel(layer, taps, first_tap, dc, a, out):
    half = taps // 2
    for at in range(out.shape[0]):
        by = -(first_tap + at - half) * DILATIONS[layer]
        total = None
        for window in range(dc.shape[0]):
            part = nt(shifted(dc[window], by), a[window])
            total = part if total is None else total + part
        out[at] = total.astype(BF)


def whole_spec(shape):
    return pl.BlockSpec(
        shape, lambda *_: (0,) * len(shape), pipeline_mode=pl.Buffered(buffer_count=1)
    )


def window_spec(shape):
    return pl.BlockSpec((1,) + shape[1:], lambda i: (i,) + (0,) * (len(shape) - 1))


def smem_spec():
    return pl.BlockSpec(memory_space=pltpu.SMEM)


def params():
    return pltpu.CompilerParams(vmem_limit_bytes=VMEM_BYTES)


def cost(flops, nbytes):
    return pl.CostEstimate(flops=int(flops), bytes_accessed=int(nbytes), transcendentals=0)


def struct(shape, dtype):
    return jax.ShapeDtypeStruct(shape, dtype)


def rotate(value, axis, ways, by):
    return lax.ppermute(value, axis, [(i, (i + by) % ways) for i in range(ways)])


def pick(value, index, dim):
    return lax.dynamic_index_in_dim(value, index, dim, keepdims=False)


def reduce_stage(value, axis, ways, dim):
    me = lax.axis_index(axis)
    total = pick(value, me, dim).astype(F32)
    for by in range(1, ways):
        got = rotate(pick(value, lax.rem(me + by, ways), dim), axis, ways, by)
        total = total + got.astype(F32)
    return total.astype(BF)


def arrange(pieces, axis, dim):
    me = lax.axis_index(axis)
    ways = len(pieces)
    if ways == 2:
        low = jnp.where(me == 0, pieces[0], pieces[1])
        high = jnp.where(me == 0, pieces[1], pieces[0])
        return jnp.stack([low, high], axis=dim)
    shape = list(pieces[0].shape)
    shape.insert(dim, ways)
    out = jnp.zeros(shape, pieces[0].dtype)
    for back, piece in enumerate(pieces):
        spot = lax.rem(me + (ways - back), ways)
        out = lax.dynamic_update_index_in_dim(out, piece, spot, dim)
    return out


def gather_stage(value, axis, ways, dim):
    pieces = [value] + [rotate(value, axis, ways, by) for by in range(1, ways)]
    return arrange(pieces, axis, dim)


def body(sizes, *args):
    (
        x_in,
        conv_w,
        conv_b,
        ln_gain,
        ln_bias,
        up_w,
        up_b,
        down_w,
        down_b,
        readout,
        cotangent,
        masked,
        species,
    ) = args
    n_z, n_y, n_core, n_tp = sizes
    layers, part, taps, size = conv_w.shape
    windows, _, length = x_in.shape
    mine = windows // n_tp
    planes = taps + 2
    me = lax.axis_index("tp")
    me_arr = jnp.full((1,), me, jnp.int32)
    row = part // (n_core * n_y * n_z)

    packs = []
    for layer in range(layers):
        packs.append(
            jnp.concatenate(
                [
                    jnp.transpose(conv_w[layer], (1, 0, 2)),
                    jnp.transpose(up_w[layer])[None],
                    down_w[layer][None],
                ]
            )
        )

    def full_weights(pack):
        cut = pack.reshape(planes, n_core, n_y, n_z, row, size)
        own = pick(
            pick(pick(cut, lax.axis_index("core"), 1), lax.axis_index("y"), 1),
            lax.axis_index("z"),
            1,
        )
        blocks = [pack]
        for by in range(1, n_tp):
            got = rotate(own, "tp", n_tp, by)
            got = gather_stage(got, "z", n_z, 1)
            got = gather_stage(got, "y", n_y, 1)
            got = gather_stage(got, "core", n_core, 1)
            blocks.append(got.reshape(planes, part, size))
        return arrange(blocks, "tp", 1).reshape(planes, size, size)

    def to_windows(value):
        cut = value.reshape(n_tp, mine, part, length)
        pieces = [pick(cut, me, 0)]
        for by in range(1, n_tp):
            pieces.append(rotate(pick(cut, lax.rem(me + by, n_tp), 0), "tp", n_tp, by))
        return pieces

    columns = []
    for layer in range(layers):
        columns += [
            conv_b[layer],
            ln_gain[layer, 0],
            ln_bias[layer, 0],
            up_b[layer],
            down_b[layer],
            ln_gain[layer, 1],
            ln_bias[layer, 1],
            jnp.zeros((part,), BF),
        ]
    table = jnp.concatenate([jnp.stack(columns), jnp.transpose(readout)])
    table = jnp.pad(table, ((0, 2), (0, 0)))
    table = gather_stage(table, "tp", n_tp, 1).reshape(table.shape[0], size)
    pc = jnp.transpose(table[: layers * COLUMNS]).astype(F32)
    read_rows = table[layers * COLUMNS :]

    x_pieces = to_windows(x_in)
    w_full = [full_weights(packs[0])]
    cot_pieces = to_windows(cotangent)
    w_full.append(full_weights(packs[1]))

    window = (mine, size, length)
    piece_shape = (mine, part, length)
    kept_struct = [struct(window, BF)] * 8
    fwd_scratch = [
        pltpu.VMEM((size, length), BF),
        pltpu.VMEM((taps, size, length), BF),
        pltpu.VMEM((size, length), F32),
        pltpu.VMEM((size, length), F32),
    ]
    conv_flops = 2.0 * taps * size * size * length * mine
    ff_flops = 4.0 * size * size * length * mine
    first = pl.pallas_call(
        functools.partial(first_kernel, 0, n_tp, taps),
        grid=(mine,),
        in_specs=[smem_spec(), whole_spec((planes, size, size)), whole_spec(pc.shape)]
        + [window_spec(piece_shape)] * n_tp,
        out_specs=[window_spec(window)] * 9,
        out_shape=kept_struct + [struct(window, BF)],
        scratch_shapes=fwd_scratch,
        compiler_params=params(),
        cost_estimate=cost(conv_flops + ff_flops, 20e6),
        name="forward_first",
    )(me_arr, w_full[0], pc, *x_pieces)
    kept0, hidden = first[:8], first[8]

    mask_rows = lax.dynamic_slice_in_dim(masked, me * mine, mine, 0).reshape(mine, 1, length)
    second = pl.pallas_call(
        functools.partial(forward_kernel, 1, 1, n_tp, taps),
        grid=(mine,),
        in_specs=[smem_spec(), whole_spec((planes, size, size)), whole_spec(pc.shape)]
        + [window_spec(window), whole_spec(read_rows.shape), window_spec((mine, 1, length))],
        out_specs=[window_spec(window)] * 8
        + [window_spec(piece_shape)] * n_tp
        + [window_spec((mine, 8, 128))],
        out_shape=kept_struct + [struct(piece_shape, BF)] * n_tp + [struct((mine, 8, 128), F32)],
        scratch_shapes=fwd_scratch,
        compiler_params=params(),
        cost_estimate=cost(conv_flops + ff_flops, 20e6),
        name="forward_second",
    )(me_arr, w_full[1], pc, hidden, read_rows, mask_rows)
    kept1, y_pieces, chance = second[:8], second[8 : 8 + n_tp], second[8 + n_tp]

    y_back = [y_pieces[0]] + [rotate(y_pieces[by], "tp", n_tp, by) for by in range(1, n_tp)]
    y_out = arrange(y_back, "tp", 0).reshape(windows, part, length)

    per_window = jnp.sum(chance, axis=2)[:, :6]
    my_species = lax.dynamic_slice_in_dim(species, me * mine, mine, 0)
    hot = (my_species[None, :] == jnp.arange(SPECIES, dtype=jnp.int32)[:, None]).astype(F32)
    species_part = jnp.dot(hot, per_window, precision=lax.Precision.HIGHEST) / length

    chain_out_specs = [
        window_spec(window),
        window_spec(window),
        whole_spec((2, size, size)),
        whole_spec((size, 128)),
    ]
    chain_out = [
        struct(window, BF),
        struct(window, BF),
        struct((2, size, size), BF),
        struct((size, 128), F32),
    ]
    chain_scratch = [
        pltpu.VMEM((size, length), F32),
        pltpu.VMEM((size, length), BF),
        pltpu.VMEM((2, size, size), F32),
        pltpu.VMEM((7, size, 128), F32),
    ]
    grad_scratch = pltpu.VMEM((size, length), F32)
    wide_scratch = pltpu.VMEM((taps, size, length), BF)
    dc1, dm1, ff1, small1 = pl.pallas_call(
        functools.partial(top_kernel, 1, n_tp, taps),
        grid=(mine,),
        in_specs=[smem_spec(), whole_spec((planes, size, size)), whole_spec(pc.shape)]
        + [window_spec(piece_shape)] * n_tp
        + [window_spec(window)] * 7,
        out_specs=chain_out_specs,
        out_shape=chain_out,
        scratch_shapes=[grad_scratch] + chain_scratch,
        compiler_params=params(),
        cost_estimate=cost(2 * ff_flops, 20e6),
        name="chain_second",
    )(me_arr, w_full[1], pc, *cot_pieces, *kept1[1:])

    def conv_weight_grad(layer, dc, a):
        return pl.pallas_call(
            functools.partial(weight_kernel, layer, taps, 0),
            in_specs=[pl.BlockSpec(memory_space=pltpu.VMEM)] * 2,
            out_specs=pl.BlockSpec(memory_space=pltpu.VMEM),
            out_shape=struct((taps, size, size), BF),
            compiler_params=params(),
            cost_estimate=cost(conv_flops, 10e6),
            name=("weights_first", "weights_second")[layer],
        )(dc, a)

    conv1 = conv_weight_grad(1, dc1, kept1[0])

    dc0, dm0, ff0, small0 = pl.pallas_call(
        functools.partial(middle_kernel, 0, taps),
        grid=(mine,),
        in_specs=[whole_spec((planes, size, size))] * 2
        + [whole_spec(pc.shape)]
        + [window_spec(window)] * 9,
        out_specs=chain_out_specs,
        out_shape=chain_out,
        scratch_shapes=[grad_scratch, wide_scratch] + chain_scratch,
        compiler_params=params(),
        cost_estimate=cost(conv_flops + 2 * ff_flops, 20e6),
        name="chain_first",
    )(w_full[1], w_full[0], pc, dc1, dm1, *kept0[1:])

    x_grads = pl.pallas_call(
        functools.partial(bottom_kernel, 0, taps, n_tp),
        grid=(mine,),
        in_specs=[smem_spec(), whole_spec((planes, size, size))] + [window_spec(window)] * 2,
        out_specs=[window_spec(piece_shape)] * n_tp,
        out_shape=[struct(piece_shape, F32)] + [struct(piece_shape, BF)] * (n_tp - 1),
        scratch_shapes=[grad_scratch, wide_scratch],
        compiler_params=params(),
        cost_estimate=cost(conv_flops, 15e6),
        name="input_grad",
    )(me_arr, w_full[0], dc0, dm0)
    x_back = [x_grads[0]] + [
        rotate(x_grads[by], "tp", n_tp, by).astype(F32) for by in range(1, n_tp)
    ]
    grad_x = arrange(x_back, "tp", 0).reshape(windows, part, length)

    conv0 = conv_weight_grad(0, dc0, kept0[0])

    def total(value):
        count, _, width = value.shape
        value = value.reshape(count, n_tp, n_core, n_y, n_z, row, width)
        value = reduce_stage(value, "core", n_core, 2)
        value = reduce_stage(value, "tp", n_tp, 1)
        value = reduce_stage(value, "y", n_y, 1)
        value = reduce_stage(value, "z", n_z, 1)
        value = gather_stage(value, "z", n_z, 1)
        value = gather_stage(value, "y", n_y, 1)
        value = gather_stage(value, "core", n_core, 1)
        return value.reshape(count, part, width)

    spread = jnp.pad(species_part.reshape(1, SPECIES * 6, 1), ((0, 0), (0, part - SPECIES * 6), (0, 0)))
    spread = jnp.broadcast_to(spread, (n_tp, part, 1)).reshape(size, 1)
    small1 = jnp.where(jnp.arange(128)[None, :] == 7, spread, small1)
    conv1_sum, ff1_sum, small1_sum = total(conv1), total(ff1), total(small1.astype(BF)[None])
    ff0_sum, small0_sum, conv0_sum = total(ff0), total(small0.astype(BF)[None]), total(conv0)

    grad_conv_w = jnp.transpose(jnp.stack([conv0_sum, conv1_sum]), (0, 2, 1, 3)).astype(F32)
    grad_up_w = jnp.stack([jnp.transpose(ff0_sum[0]), jnp.transpose(ff1_sum[0])]).astype(F32)
    grad_down_w = jnp.stack([ff0_sum[1], ff1_sum[1]]).astype(F32)
    smalls = jnp.transpose(jnp.concatenate([small0_sum, small1_sum]), (0, 2, 1)).astype(F32)
    species_sum = smalls[1, 7, : SPECIES * 6].reshape(SPECIES, 6)
    return (
        y_out,
        grad_x,
        grad_conv_w,
        smalls[:, CONV_B],
        jnp.stack([smalls[:, GAIN_A], smalls[:, GAIN_B]], axis=1),
        jnp.stack([smalls[:, BIAS_A], smalls[:, BIAS_B]], axis=1),
        grad_up_w,
        smalls[:, UP_B],
        grad_down_w,
        smalls[:, DOWN_B],
        species_sum,
    )


def solution(mesh):
    dp, tp = mesh.shape["dp"], mesh.shape["tp"]
    n_core = n_y = 2
    n_z = dp // (n_core * n_y)
    fine = Mesh(mesh.devices.reshape(n_z, n_y, n_core, tp), DP + ("tp",))
    placed = (
        P(DP, "tp", None),
        P(None, "tp", None, None),
        P(None, "tp"),
        P(None, None, "tp"),
        P(None, None, "tp"),
        P(None, None, "tp"),
        P(None, "tp"),
        P(None, "tp", None),
        P(None, "tp"),
        P("tp", None),
        P(DP, "tp", None),
        P(DP, None),
        P(DP),
    )
    return jax.shard_map(
        functools.partial(body, (n_z, n_y, n_core, tp)),
        mesh=fine,
        in_specs=placed,
        out_specs=(
            P(DP, "tp", None),
            P(DP, "tp", None),
            P(None, "tp", None, None),
            P(None, "tp"),
            P(None, None, "tp"),
            P(None, None, "tp"),
            P(None, None, "tp"),
            P(None, "tp"),
            P(None, "tp", None),
            P(None, "tp"),
            P(),
        ),
        check_vma=False,
    )
```

time: 1590 us -> 544 us (0.34)
  waiting for transfers between devices: 973 us -> 214 us
  matrix products: 279 us -> 0.12 us
  other arithmetic: 188 us -> 40.9 us
  Pallas kernels: 0 us -> 147 us
  starting transfers between devices: 0.99 us -> 90.6 us
  blocking collectives: 85.3 us -> 0 us
    reduce_scatter x6 -> x0, waiting for transfers between devices: 557 us -> none  [the longest x4 362 us: input_sum(): return lax.psum_scatter(tensor, 'tp', scatter_dimension=2, tiled=True)]
    all_gather x6 -> x0, waiting for transfers between devices: 337 us -> none  [the longest x4 222 us: gather_rows(): return lax.all_gather(tensor, 'tp', axis=2, tiled=True)]
    dot_general x68 -> x1, matrix products: 279 us -> 0.12 us  [body(): jnp.dot(hot, per_window, precision=lax.Precision.HIGHEST) / length]
    ppermute x0 -> x83, waiting for transfers between devices: none -> 214 us  [rotate(): lax.ppermute(value, axis, [(i, (i + by) % ways) for i in range(ways)])]
    pallas_call x0 -> x7, Pallas kernels: none -> 147 us  [the longest x1 29.5 us: body(): pl.pallas_call(functools.partial(forward_kernel, 1, 1, n_tp, taps), grid=...]
    reduce_sum x15 -> x1, other arithmetic: 124 us -> 0.09 us  [body(): per_window = jnp.sum(chance, axis=2)[:, :6]]
    ppermute x0 -> x83, starting transfers between devices: none -> 90.6 us  [rotate(): lax.ppermute(value, axis, [(i, (i + by) % ways) for i in range(ways)])]
    psum x8 -> x0, blocking collectives: 85.3 us -> none  [the longest x1 34.6 us: body(): lax.psum(stacked_tensor[1].astype(jnp.bfloat16), 'dp').astype(jnp.float32)]
  transfers between devices with their start and end apart: 14 -> 83, of which waited for: 14 -> 44; matrix products, arithmetic and copies ran while one was open for 6% -> 12% of each run, Pallas kernels for 0% -> 19%
where the time goes in v1:
time: 544 us; the launch traced here: 540 us
  waiting for transfers between devices  214 us (39%)
  Pallas kernels  147 us (27%)
  starting transfers between devices  90.6 us (17%)
  local copies, waits for them, and re-layouts  44.9 us (8%)
  other arithmetic  40.9 us (8%)
    ppermute x83, waiting for transfers between devices, rotate(): lax.ppermute(value, axis, [(i, (i + by) % ways) for i in range(ways)])  214 us
    ppermute x83, starting transfers between devices, rotate(): lax.ppermute(value, axis, [(i, (i + by) % ways) for i in range(ways)])  90.6 us
    pallas_call x1, Pallas kernels, body(): pl.pallas_call(functools.partial(forward_kernel, 1, 1, n_tp, taps), grid=...  29.5 us
    pallas_call x1, Pallas kernels, body(): pl.pallas_call(functools.partial(middle_kernel, 0, taps), grid=(mine,), i...  29.3 us
    pallas_call x2, Pallas kernels, conv_weight_grad(): pl.pallas_call(functools.partial(weight_kernel, layer, taps, 0), in_specs...  28.8 us
    pallas_call x1, Pallas kernels, body(): pl.pallas_call(functools.partial(first_kernel, 0, n_tp, taps), grid=(mine...  27.3 us
    another operation x40, other arithmetic, arrange(): return jnp.stack([low, high], axis=dim)  21.6 us
    pallas_call x1, Pallas kernels, body(): pl.pallas_call(functools.partial(top_kernel, 1, n_tp, taps), grid=(mine,)...  16.5 us
  transfers between devices with their start and end apart: 83, of which 44 were waited for; matrix products, arithmetic and copies ran while one was open for 12% of the time, Pallas kernels for 19%

profile of v1, /device:TPU:0, one launch (start us, length us, event | category | flops | bytes accessed | tf_op | source)
XLA Modules:
  0.0 539.8 jit_solution(12216524319234395520)
XLA Ops:
  0.7 5.9 %slice_bitcast_fusion.10 = (bf16[9,1,256,512]{3,2,0,1:T(8,128)(2,1)}, bf16[9,1,256,512]{3,2,0,1:T(8,128)(2,1)}, bf16[1,256,9,512]{3,1,2,0:T(8,128)(2,1)}, bf16[1,256,9,512]{3,1,2,0:T(8,128)(2,1)S(1)}) fusion(bf16[2,256,9,512]{3,1,2,0:T(8,128)(2,1)} %param.14), kind=kLoop, calls=%fused_computation.271 | loop fusion | bytes 14155776 | tf_op jit(solution)/shard_map/concatenate | solution.py:393
  10.1 2.9 collective-permute-start.7
  13.0 3.0 dynamic-slice_bitcast_fusion.6
  24.1 20.7 %collective-permute-done = bf16[11,16,512]{2,1,0:T(8,128)(2,1)S(1)} collective-permute-done((bf16[11,16,512]{2,1,0:T(8,128)(2,1)S(1)}, bf16[11,16,512]{2,1,0:T(8,128)(2,1)S(1)}, u32[]{:S(2)}, u32[]{:S(2)}) %collective-permute-start) | collective-permute-done | bytes 180256 | tf_op jit(solution)/shard_map/ppermute | solution.py:328
  53.9 6.0 %collective-permute-done.2 = bf16[11,16,512]{2,1,0:T(8,128)(2,1)S(1)} collective-permute-done((bf16[11,16,512]{2,1,0:T(8,128)(2,1)S(1)}, bf16[11,16,512]{2,1,0:T(8,128)(2,1)S(1)}, u32[]{:S(2)}, u32[]{:S(2)}) %collective-permute-start.2) | collective-permute-done | bytes 180256 | tf_op jit(solution)/shard_map/ppermute | solution.py:328
  61.5 9.4 %collective-permute-done.11 = bf16[11,4,16,512]{3,2,1,0:T(8,128)(2,1)S(1)} collective-permute-done((bf16[11,4,16,512]{3,2,1,0:T(8,128)(2,1)S(1)}, bf16[11,4,16,512]{3,2,1,0:T(8,128)(2,1)S(1)}, u32[]{:S(2)}, u32[]{:S(2)}) %collective-permute-start.11) | collective-permute-done | bytes 720928 | tf_op jit(solution)/shard_map/ppermute | solution.py:328
  73.6 3.0 dynamic-slice_bitcast_fusion.4
  78.3 5.0 collective-permute-done.4
  93.5 2.8 copy.209
  99.3 2.9 copy.198
  102.2 27.3 %forward_first.1 = (bf16[4,512,512]{2,1,0:T(8,128)(2,1)}, bf16[4,512,512]{2,1,0:T(8,128)(2,1)}, bf16[4,512,512]{2,1,0:T(8,128)(2,1)}, bf16[4,512,512]{2,1,0:T(8,...) custom-call(s32[1]{0:T(128)} %bitcast.refs_0_, ...), custom_call_target="tpu_custom_call" | custom-call | flops 11811160064 | bytes 20000000 | tf_op jit(solution)/shard_map/forward_first/pallas_call | solution.py:459
  129.5 29.5 %forward_second.1 = (bf16[4,512,512]{2,1,0:T(8,128)(2,1)}, bf16[4,512,512]{2,1,0:T(8,128)(2,1)}, bf16[4,512,512]{2,1,0:T(8,128)(2,1)}, bf16[4,512,512]{2,1,0:T(8...) custom-call(s32[1]{0:T(128)} %bitcast.refs_0_, ...), custom_call_target="tpu_custom_call" | custom-call | flops 11811160064 | bytes 20000000 | tf_op jit(solution)/shard_map/forward_second/pallas_call | solution.py:474
  159.0 16.5 %chain_second.1 = (bf16[4,512,512]{2,1,0:T(8,128)(2,1)}, bf16[4,512,512]{2,1,0:T(8,128)(2,1)}, bf16[2,512,512]{2,1,0:T(8,128)(2,1)}, f32[512,128]{1,0:T(8,128)}) custom-call(s32[1]{0:T(128)} %bitcast.refs_0_, bf16[11,512,512]{2,1,0:T(8,128)(2,1)} %bitcast.489, f32[512,16]{1,0:T(8,128)} %bitcast.518, bf16[4,256,512]{2,1,0:T(8,128)(2,1)} %get-tuple-element.149.refs_3_, ...), custom_call_target="tpu_custom_call" | custom-call | flops 4294967296 | bytes 20000000 | tf_op jit(solution)/shard_map/chain_second/pallas_call | solution.py:518
  175.5 29.3 %chain_first.1 = (bf16[4,512,512]{2,1,0:T(8,128)(2,1)}, bf16[4,512,512]{2,1,0:T(8,128)(2,1)}, bf16[2,512,512]{2,1,0:T(8,128)(2,1)}, f32[512,128]{1,0:T(8,128)}) custom-call(bf16[11,512,512]{2,1,0:T(8,128)(2,1)} %bitcast.490, bf16[11,512,512]{2,1,0:T(8,128)(2,1)} %bitcast.498, f32[512,16]{1,0:T(8,128)} %bitcast.519, ...), custom_call_target="tpu_custom_call" | custom-call | flops 13958643712 | bytes 20000000 | tf_op jit(solution)/shard_map/chain_first/pallas_call | solution.py:545
  210.6 14.3 %weights_first.1 = bf16[9,512,512]{2,1,0:T(8,128)(2,1)} custom-call(bf16[4,512,512]{2,1,0:T(8,128)(2,1)} %get-tuple-element.60.refs_2_.dc, bf16[4,512,512]{2,1,0:T(8,128)(2,1)} %get-tuple-element.64.a), custom_call_target="tpu_custom_call" | custom-call | flops 9663676416 | bytes 10000000 | tf_op jit(solution)/shard_map/weights_first/pallas_call | solution.py:533
  224.9 3.4 dynamic-slice_bitcast_fusion.1
  228.3 14.6 %weights_second.1 = bf16[9,512,512]{2,1,0:T(8,128)(2,1)} custom-call(bf16[4,512,512]{2,1,0:T(8,128)(2,1)} %get-tuple-element.51.refs_3_.dc, bf16[4,512,512]{2,1,0:T(8,128)(2,1)} %get-tuple-element.65.a), custom_call_target="tpu_custom_call" | custom-call | flops 9663676416 | bytes 10000000 | tf_op jit(solution)/shard_map/weights_second/pallas_call | solution.py:533
  242.9 15.9 %input_grad.1 = (f32[4,256,512]{2,1,0:T(8,128)}, bf16[4,256,512]{2,1,0:T(8,128)(2,1)}) custom-call(s32[1]{0:T(128)} %bitcast.refs_0_, bf16[11,512,512]{2,1,0:T(8,128)(2,1)} %bitcast.499, bf16[4,512,512]{2,1,0:T(8,128)(2,1)} %get-tuple-element.60.refs_2_.dc, bf16[4,512,512]{2,1,0:T(8,128)(2,1)} %get-tuple-element.61.refs_3_), custom_call_target="tpu_custom_call" | custom-call | flops 9663676416 | bytes 15000000 | tf_op jit(solution)/shard_map/input_grad/pallas_call | solution.py:559
  274.5 3.3 collective-permute-start.55
  281.9 3.4 collective-permute-done.45
  285.3 4.5 collective-permute-done.46
  293.6 5.2 collective-permute-done.56
  298.8 4.5 collective-permute-done.57
  329.5 5.8 %collective-permute-done.62 = bf16[2,2,4,16,512]{4,3,0,2,1:T(8,128)(2,1)S(1)} collective-permute-done((bf16[2,2,4,16,512]{4,3,0,2,1:T(8,128)(2,1)S(1)}, bf16[2,2,4,16,512]{4,3,0,2,1:T(8,128)(2,1)S(1)}, u32[]{:S(2)}, u32[]{:S(2)}) %collective-permute-start.62) | collective-permute-done | bytes 262176 | tf_op jit(solution)/shard_map/ppermute | solution.py:328
  337.0 3.1 collective-permute-done.73
  342.0 3.9 collective-permute-start.65
  345.8 2.8 collective-permute-start.66
  351.0 3.4 collective-permute-start.77
  357.1 5.1 collective-permute-done.67
  362.3 4.8 collective-permute-done.68
  371.2 5.7 %collective-permute-done.78 = bf16[2,16,512]{2,1,0:T(8,128)(2,1)S(1)} collective-permute-done((bf16[2,16,512]{2,1,0:T(8,128)(2,1)S(1)}, bf16[2,16,512]{2,1,0:T(8,128)(2,1)S(1)}, u32[]{:S(2)}, u32[]{:S(2)}) %collective-permute-start.78) | collective-permute-done | bytes 32800 | tf_op jit(solution)/shard_map/ppermute | solution.py:328
  377.1 4.6 collective-permute-done.79
  388.4 3.2 fusion.1
  395.2 7.8 %collective-permute-done.14 = bf16[4,256,512]{2,1,0:T(8,128)(2,1)S(1)} collective-permute-done((bf16[4,256,512]{2,1,0:T(8,128)(2,1)S(1)}, bf16[4,256,512]{2,1,0:T(8,128)(2,1)S(1)}, u32[]{:S(2)}, u32[]{:S(2)}) %collective-permute-start.14) | collective-permute-done | bytes 1048608 | tf_op jit(solution)/shard_map/ppermute | solution.py:328
  407.3 21.0 %collective-permute-done.18 = bf16[9,2,4,16,512]{4,3,2,1,0:T(8,128)(2,1)S(1)} collective-permute-done((bf16[9,2,4,16,512]{4,3,2,1,0:T(8,128)(2,1)S(1)}, bf16[9,2,4,16,512]{4,3,2,1,0:T(8,128)(2,1)S(1)}, u32[]{:S(2)}, u32[]{:S(2)}) %collective-permute-start.18) | collective-permute-done | bytes 1179680 | tf_op jit(solution)/shard_map/ppermute | solution.py:328
  430.5 19.1 %collective-permute-done.29 = bf16[9,2,4,16,512]{4,3,2,1,0:T(8,128)(2,1)S(1)} collective-permute-done((bf16[9,2,4,16,512]{4,3,2,1,0:T(8,128)(2,1)S(1)}, bf16[9,2,4,16,512]{4,3,2,1,0:T(8,128)(2,1)S(1)}, u32[]{:S(2)}, u32[]{:S(2)}) %collective-permute-start.29) | collective-permute-done | bytes 1179680 | tf_op jit(solution)/shard_map/ppermute | solution.py:328
  452.8 8.8 %collective-permute-done.30 = bf16[9,4,16,512]{3,2,1,0:T(8,128)(2,1)S(1)} collective-permute-done((bf16[9,4,16,512]{3,2,1,0:T(8,128)(2,1)S(1)}, bf16[9,4,16,512]{3,2,1,0:T(8,128)(2,1)S(1)}, u32[]{:S(2)}, u32[]{:S(2)}) %collective-permute-start.30) | collective-permute-done | bytes 589856 | tf_op jit(solution)/shard_map/ppermute | solution.py:328
  463.9 3.2 collective-permute-done.21
  470.9 5.3 collective-permute-start.23
  476.2 3.2 collective-permute-done.32
  479.4 5.0 collective-permute-done.33
  484.6 4.2 collective-permute-start.34
  488.8 3.2 collective-permute-done.24
  492.1 5.0 collective-permute-done.25
  498.0 5.8 %collective-permute-done.35 = bf16[9,16,512]{2,1,0:T(8,128)(2,1)S(1)} collective-permute-done((bf16[9,16,512]{2,1,0:T(8,128)(2,1)S(1)}, bf16[9,16,512]{2,1,0:T(8,128)(2,1)S(1)}, u32[]{:S(2)}, u32[]{:S(2)}) %collective-permute-start.35) | collective-permute-done | bytes 147488 | tf_op jit(solution)/shard_map/ppermute | solution.py:328
  507.5 5.8 %collective-permute-done.26 = bf16[9,4,16,512]{3,2,1,0:T(8,128)(2,1)S(1)} collective-permute-done((bf16[9,4,16,512]{3,2,1,0:T(8,128)(2,1)S(1)}, bf16[9,4,16,512]{3,2,1,0:T(8,128)(2,1)S(1)}, u32[]{:S(2)}, u32[]{:S(2)}) %collective-permute-start.26) | collective-permute-done | bytes 589856 | tf_op jit(solution)/shard_map/ppermute | solution.py:328
  514.6 10.5 %collective-permute-done.37 = bf16[9,4,16,512]{3,2,1,0:T(8,128)(2,1)S(1)} collective-permute-done((bf16[9,4,16,512]{3,2,1,0:T(8,128)(2,1)S(1)}, bf16[9,4,16,512]{3,2,1,0:T(8,128)(2,1)S(1)}, u32[]{:S(2)}, u32[]{:S(2)}) %collective-permute-start.37) | collective-permute-done | bytes 589856 | tf_op jit(solution)/shard_map/ppermute | solution.py:328
  535.0 4.4 convert_bitcast_fusion
  (360 shorter events, 149.5 us)
Async XLA Ops:
  10.1 8.5 %collective-permute-start.7 = (bf16[11,16,512]{2,1,0:T(8,128)(2,1)}, bf16[11,16,512]{2,1,0:T(8,128)(2,1)}, u32[]{:S(2)}, u32[]{:S(2)}) collective-permute-start(bf16[11,16,512]{2,1,0:T(8,128)(2,1)} %fusion.27), channel_id=1, source_target_pairs={{0,1},{1,0},{2,3},{3,2},{4,5},{5,4},{6,7},{7,6},{8,9},{9,8},{10,11... | collective-permute-start | bytes 540680 | tf_op jit(solution)/shard_map/ppermute | solution.py:328
  16.0 86.2 %collective-permute-start.13 = (bf16[4,256,512]{2,1,0:T(8,128)(2,1)}, bf16[4,256,512]{2,1,0:T(8,128)(2,1)}, u32[]{:S(2)}, u32[]{:S(2)}) collective-permute-start(bf16[4,256,512]{2,1,0:T(8,128)(2,1)} %get-tuple-element.152), channel_id=1, source_target_pairs={{0,1},{1,0},{2,3},{3,2},{4,5},{5,4},{6,7},{7,6},{8,9},{9,8},{10,11... | collective-permute-start | bytes 3145736 | tf_op jit(solution)/shard_map/ppermute | solution.py:328
  16.3 28.5 %collective-permute-start = (bf16[11,16,512]{2,1,0:T(8,128)(2,1)S(1)}, bf16[11,16,512]{2,1,0:T(8,128)(2,1)S(1)}, u32[]{:S(2)}, u32[]{:S(2)}) collective-permute-start(bf16[11,16,512]{2,1,0:T(8,128)(2,1)S(1)} %fusion.26), channel_id=1, source_target_pairs={{0,1},{1,0},{2,3},{3,2},{4,5},{5,4},{6,7},{7,6},{8,9},{9,8},{10,11... | collective-permute-start | bytes 540680 | tf_op jit(solution)/shard_map/ppermute | solution.py:328
  18.5 28.9 %collective-permute-start.8 = (bf16[11,16,512]{2,1,0:T(8,128)(2,1)}, bf16[11,16,512]{2,1,0:T(8,128)(2,1)S(1)}, u32[]{:S(2)}, u32[]{:S(2)}) collective-permute-start(bf16[11,16,512]{2,1,0:T(8,128)(2,1)} %collective-permute-done.7), channel_id=1, source_target_pairs={{0,8},{8,16},{16,24},{24,0},{1,9},{9,17},{17,25},{25,1},{2,10},{10... | collective-permute-start | bytes 540680 | tf_op jit(solution)/shard_map/ppermute | solution.py:328
  20.1 29.9 %collective-permute-start.9 = (bf16[11,16,512]{2,1,0:T(8,128)(2,1)}, bf16[11,16,512]{2,1,0:T(8,128)(2,1)S(1)}, u32[]{:S(2)}, u32[]{:S(2)}) collective-permute-start(bf16[11,16,512]{2,1,0:T(8,128)(2,1)} %collective-permute-done.7), channel_id=1, source_target_pairs={{0,16},{8,24},{16,0},{24,8},{1,17},{9,25},{17,1},{25,9},{2,18},{10... | collective-permute-start | bytes 540680 | tf_op jit(solution)/shard_map/ppermute | solution.py:328
  22.7 29.0 %collective-permute-start.10 = (bf16[11,16,512]{2,1,0:T(8,128)(2,1)}, bf16[11,16,512]{2,1,0:T(8,128)(2,1)S(1)}, u32[]{:S(2)}, u32[]{:S(2)}) collective-permute-start(bf16[11,16,512]{2,1,0:T(8,128)(2,1)} %collective-permute-done.7), channel_id=1, source_target_pairs={{0,24},{8,0},{16,8},{24,16},{1,25},{9,1},{17,9},{25,17},{2,26},{10... | collective-permute-start | bytes 540680 | tf_op jit(solution)/shard_map/ppermute | solution.py:328
  44.8 9.0 %collective-permute-start.1 = (bf16[11,16,512]{2,1,0:T(8,128)(2,1)S(1)}, bf16[11,16,512]{2,1,0:T(8,128)(2,1)S(1)}, u32[]{:S(2)}, u32[]{:S(2)}) collective-permute-start(bf16[11,16,512]{2,1,0:T(8,128)(2,1)S(1)} %collective-permute-done), channel_id=1, source_target_pairs={{0,8},{8,16},{16,24},{24,0},{1,9},{9,17},{17,25},{25,1},{2,10},{10... | collective-permute-start | bytes 540680 | tf_op jit(solution)/shard_map/ppermute | solution.py:328
  47.4 12.4 %collective-permute-start.2 = (bf16[11,16,512]{2,1,0:T(8,128)(2,1)S(1)}, bf16[11,16,512]{2,1,0:T(8,128)(2,1)S(1)}, u32[]{:S(2)}, u32[]{:S(2)}) collective-permute-start(bf16[11,16,512]{2,1,0:T(8,128)(2,1)S(1)} %collective-permute-done), channel_id=1, source_target_pairs={{0,16},{8,24},{16,0},{24,8},{1,17},{9,25},{17,1},{25,9},{2,18},{10... | collective-permute-start | bytes 540680 | tf_op jit(solution)/shard_map/ppermute | solution.py:328
  50.1 9.8 %collective-permute-start.3 = (bf16[11,16,512]{2,1,0:T(8,128)(2,1)S(1)}, bf16[11,16,512]{2,1,0:T(8,128)(2,1)S(1)}, u32[]{:S(2)}, u32[]{:S(2)}) collective-permute-start(bf16[11,16,512]{2,1,0:T(8,128)(2,1)S(1)} %collective-permute-done), channel_id=1, source_target_pairs={{0,24},{8,0},{16,8},{24,16},{1,25},{9,1},{17,9},{25,17},{2,26},{10... | collective-permute-start | bytes 540680 | tf_op jit(solution)/shard_map/ppermute | solution.py:328
  51.8 19.1 %collective-permute-start.11 = (bf16[11,4,16,512]{3,2,1,0:T(8,128)(2,1)S(1)}, bf16[11,4,16,512]{3,2,1,0:T(8,128)(2,1)S(1)}, u32[]{:S(2)}, u32[]{:S(2)}) collective-permute-start(bf16[11,4,16,512]{3,2,1,0:T(8,128)(2,1)S(1)} %bitcast_dynamic-update-slice_fusion.6), channel_id=1, source_target_pairs={{0,4},{4,0},{1,5},{5,1},{2,6},{6,2},{3,7},{7,3},{8,12},{12,8},{9,1... | collective-permute-start | bytes 2162696 | tf_op jit(solution)/shard_map/ppermute | solution.py:328
  59.9 23.3 %collective-permute-start.4 = (bf16[11,4,16,512]{3,2,1,0:T(8,128)(2,1)S(1)}, bf16[11,4,16,512]{3,2,1,0:T(8,128)(2,1)}, u32[]{:S(2)}, u32[]{:S(2)}) collective-permute-start(bf16[11,4,16,512]{3,2,1,0:T(8,128)(2,1)S(1)} %bitcast_dynamic-update-slice_fusion.3), channel_id=1, source_target_pairs={{0,4},{4,0},{1,5},{5,1},{2,6},{6,2},{3,7},{7,3},{8,12},{12,8},{9,1... | collective-permute-start | bytes 2162696 | tf_op jit(solution)/shard_map/ppermute | solution.py:328
  72.4 15.0 %collective-permute-start.12 = (bf16[11,2,4,16,512]{4,3,2,1,0:T(8,128)(2,1)}, bf16[11,2,4,16,512]{4,3,2,1,0:T(8,128)(2,1)}, u32[]{:S(2)}, u32[]{:S(2)}) collective-permute-start(bf16[11,2,4,16,512]{4,3,2,1,0:T(8,128)(2,1)} %pad_maximum_fusion.11), channel_id=1, source_target_pairs={{0,2},{2,0},{1,3},{3,1},{4,6},{6,4},{5,7},{7,5},{8,10},{10,8},{9,1... | collective-permute-start | bytes 4325384 | tf_op jit(solution)/shard_map/ppermute | solution.py:328
  72.5 13.4 %collective-permute-start.6 = (bf16[24,256]{1,0:T(8,128)(2,1)S(1)}, bf16[24,256]{1,0:T(8,128)(2,1)S(1)}, u32[]{:S(2)}, u32[]{:S(2)}) collective-permute-start(bf16[24,256]{1,0:T(8,128)(2,1)S(1)} %pad.8), channel_id=1, source_target_pairs={{0,1},{1,0},{2,3},{3,2},{4,5},{5,4},{6,7},{7,6},{8,9},{9,8},{10,11... | collective-permute-start | bytes 36872 | tf_op jit(solution)/shard_map/ppermute | solution.py:328
  76.6 82.4 %collective-permute-start.15 = (bf16[4,256,512]{2,1,0:T(8,128)(2,1)}, bf16[4,256,512]{2,1,0:T(8,128)(2,1)}, u32[]{:S(2)}, u32[]{:S(2)}) collective-permute-start(bf16[4,256,512]{2,1,0:T(8,128)(2,1)} %get-tuple-element.148), channel_id=1, source_target_pairs={{0,1},{1,0},{2,3},{3,2},{4,5},{5,4},{6,7},{7,6},{8,9},{9,8},{10,11... | collective-permute-start | bytes 3145736 | tf_op jit(solution)/shard_map/ppermute | solution.py:328
  207.0 117.6 %collective-permute-start.61 = (bf16[2,2,2,4,16,512]{5,4,0,3,2,1:T(8,128)(2,1)}, bf16[2,2,2,4,16,512]{5,4,0,3,2,1:T(8,128)(2,1)}, u32[]{:S(2)}, u32[]{:S(2)}) collective-permute-start(bf16[2,2,2,4,16,512]{5,4,0,3,2,1:T(8,128)(2,1)} %bitcast.487), channel_id=1, source_target_pairs={{0,2},{2,0},{1,3},{3,1},{4,6},{6,4},{5,7},{7,5},{8,10},{10,8},{9,1... | collective-permute-start | bytes 1572872 | tf_op jit(solution)/shard_map/ppermute | solution.py:328
  208.3 119.5 %collective-permute-start.72 = (bf16[2,2,2,4,16,512]{5,4,0,3,2,1:T(8,128)(2,1)}, bf16[2,2,2,4,16,512]{5,4,0,3,2,1:T(8,128)(2,1)}, u32[]{:S(2)}, u32[]{:S(2)}) collective-permute-start(bf16[2,2,2,4,16,512]{5,4,0,3,2,1:T(8,128)(2,1)} %bitcast.486), channel_id=1, source_target_pairs={{0,2},{2,0},{1,3},{3,1},{4,6},{6,4},{5,7},{7,5},{8,10},{10,8},{9,1... | collective-permute-start | bytes 1572872 | tf_op jit(solution)/shard_map/ppermute | solution.py:328
  209.0 51.5 %collective-permute-start.39 = (bf16[1,2,2,4,16,128]{5,4,3,2,1,0:T(8,128)(2,1)}, bf16[1,2,2,4,16,128]{5,4,3,2,1,0:T(8,128)(2,1)S(1)}, u32[]{:S(2)}, u32[]{:S(2)}) collective-permute-start(bf16[1,2,2,4,16,128]{5,4,3,2,1,0:T(8,128)(2,1)} %dynamic-slice_bitcast_fusion.21), channel_id=1, source_target_pairs={{0,2},{2,0},{1,3},{3,1},{4,6},{6,4},{5,7},{7,5},{8,10},{10,8},{9,1... | collective-permute-start | bytes 196616 | tf_op jit(solution)/shard_map/ppermute | solution.py:328
  210.6 51.5 %collective-permute-start.50 = (bf16[1,2,2,4,16,128]{5,4,3,2,1,0:T(8,128)(2,1)}, bf16[1,2,2,4,16,128]{5,4,3,2,1,0:T(8,128)(2,1)S(1)}, u32[]{:S(2)}, u32[]{:S(2)}) collective-permute-start(bf16[1,2,2,4,16,128]{5,4,3,2,1,0:T(8,128)(2,1)} %dynamic-slice_bitcast_fusion.20), channel_id=1, source_target_pairs={{0,2},{2,0},{1,3},{3,1},{4,6},{6,4},{5,7},{7,5},{8,10},{10,8},{9,1... | collective-permute-start | bytes 196616 | tf_op jit(solution)/shard_map/ppermute | solution.py:328
  279.3 109.1 %collective-permute-start.17 = (bf16[9,2,2,4,16,512]{5,4,3,2,1,0:T(8,128)(2,1)}, bf16[9,2,2,4,16,512]{5,4,3,2,1,0:T(8,128)(2,1)}, u32[]{:S(2)}, u32[]{:S(2)}) collective-permute-start(bf16[9,2,2,4,16,512]{5,4,3,2,1,0:T(8,128)(2,1)} %dynamic-slice_bitcast_fusion.1), channel_id=1, source_target_pairs={{0,2},{2,0},{1,3},{3,1},{4,6},{6,4},{5,7},{7,5},{8,10},{10,8},{9,1... | collective-permute-start | bytes 7077896 | tf_op jit(solution)/shard_map/ppermute | solution.py:328
  279.3 114.3 %collective-permute-start.28 = (bf16[9,2,2,4,16,512]{5,4,3,2,1,0:T(8,128)(2,1)}, bf16[9,2,2,4,16,512]{5,4,3,2,1,0:T(8,128)(2,1)S(1)}, u32[]{:S(2)}, u32[]{:S(2)}) collective-permute-start(bf16[9,2,2,4,16,512]{5,4,3,2,1,0:T(8,128)(2,1)} %dynamic-slice_bitcast_fusion), channel_id=1, source_target_pairs={{0,2},{2,0},{1,3},{3,1},{4,6},{6,4},{5,7},{7,5},{8,10},{10,8},{9,1... | collective-permute-start | bytes 7077896 | tf_op jit(solution)/shard_map/ppermute | solution.py:328
  326.0 9.2 %collective-permute-start.62 = (bf16[2,2,4,16,512]{4,3,0,2,1:T(8,128)(2,1)S(1)}, bf16[2,2,4,16,512]{4,3,0,2,1:T(8,128)(2,1)S(1)}, u32[]{:S(2)}, u32[]{:S(2)}) collective-permute-start(bf16[2,2,4,16,512]{4,3,0,2,1:T(8,128)(2,1)S(1)} %dynamic-slice_bitcast_fusion.11), channel_id=1, source_target_pairs={{0,1},{1,0},{2,3},{3,2},{4,5},{5,4},{6,7},{7,6},{8,9},{9,8},{10,11... | collective-permute-start | bytes 786440 | tf_op jit(solution)/shard_map/ppermute | solution.py:328
  329.2 10.9 %collective-permute-start.73 = (bf16[2,2,4,16,512]{4,3,0,2,1:T(8,128)(2,1)S(1)}, bf16[2,2,4,16,512]{4,3,0,2,1:T(8,128)(2,1)S(1)}, u32[]{:S(2)}, u32[]{:S(2)}) collective-permute-start(bf16[2,2,4,16,512]{4,3,0,2,1:T(8,128)(2,1)S(1)} %dynamic-slice_bitcast_fusion.10), channel_id=1, source_target_pairs={{0,1},{1,0},{2,3},{3,2},{4,5},{5,4},{6,7},{7,6},{8,9},{9,8},{10,11... | collective-permute-start | bytes 786440 | tf_op jit(solution)/shard_map/ppermute | solution.py:328
  348.7 7.5 %collective-permute-start.76 = (bf16[2,16,512]{2,1,0:T(8,128)(2,1)S(1)}, bf16[2,16,512]{2,1,0:T(8,128)(2,1)S(1)}, u32[]{:S(2)}, u32[]{:S(2)}) collective-permute-start(bf16[2,16,512]{2,1,0:T(8,128)(2,1)S(1)} %get-tuple-element.202), channel_id=1, source_target_pairs={{0,16},{8,24},{16,0},{24,8},{1,17},{9,25},{17,1},{25,9},{2,18},{10... | collective-permute-start | bytes 98312 | tf_op jit(solution)/shard_map/ppermute | solution.py:328
  354.4 32.7 %collective-permute-start.16 = (bf16[4,256,512]{2,1,0:T(8,128)(2,1)S(1)}, bf16[4,256,512]{2,1,0:T(8,128)(2,1)S(1)}, u32[]{:S(2)}, u32[]{:S(2)}) collective-permute-start(bf16[4,256,512]{2,1,0:T(8,128)(2,1)S(1)} %copy-done.24), channel_id=1, source_target_pairs={{0,1},{1,0},{2,3},{3,2},{4,5},{5,4},{6,7},{7,6},{8,9},{9,8},{10,11... | collective-permute-start | bytes 3145736 | tf_op jit(solution)/shard_map/ppermute | solution.py:328
  356.2 46.8 %collective-permute-start.14 = (bf16[4,256,512]{2,1,0:T(8,128)(2,1)S(1)}, bf16[4,256,512]{2,1,0:T(8,128)(2,1)S(1)}, u32[]{:S(2)}, u32[]{:S(2)}) collective-permute-start(bf16[4,256,512]{2,1,0:T(8,128)(2,1)S(1)} %copy-done.23), channel_id=1, source_target_pairs={{0,1},{1,0},{2,3},{3,2},{4,5},{5,4},{6,7},{7,6},{8,9},{9,8},{10,11... | collective-permute-start | bytes 3145736 | tf_op jit(solution)/shard_map/ppermute | solution.py:328
  385.6 21.5 %collective-permute-start.70 = (bf16[2,4,16,512]{3,2,1,0:T(8,128)(2,1)S(1)}, bf16[2,4,16,512]{3,2,1,0:T(8,128)(2,1)S(1)}, u32[]{:S(2)}, u32[]{:S(2)}) collective-permute-start(bf16[2,4,16,512]{3,2,1,0:T(8,128)(2,1)S(1)} %bitcast_dynamic-update-slice_fusion.23), channel_id=1, source_target_pairs={{0,4},{4,0},{1,5},{5,1},{2,6},{6,2},{3,7},{7,3},{8,12},{12,8},{9,1... | collective-permute-start | bytes 393224 | tf_op jit(solution)/shard_map/ppermute | solution.py:328
  387.2 64.2 %collective-permute-start.81 = (bf16[2,4,16,512]{3,2,1,0:T(8,128)(2,1)S(1)}, bf16[2,4,16,512]{3,2,1,0:T(8,128)(2,1)S(1)}, u32[]{:S(2)}, u32[]{:S(2)}) collective-permute-start(bf16[2,4,16,512]{3,2,1,0:T(8,128)(2,1)S(1)} %bitcast_dynamic-update-slice_fusion.16), channel_id=1, source_target_pairs={{0,4},{4,0},{1,5},{5,1},{2,6},{6,2},{3,7},{7,3},{8,12},{12,8},{9,1... | collective-permute-start | bytes 393224 | tf_op jit(solution)/shard_map/ppermute | solution.py:328
  391.8 36.5 %collective-permute-start.18 = (bf16[9,2,4,16,512]{4,3,2,1,0:T(8,128)(2,1)S(1)}, bf16[9,2,4,16,512]{4,3,2,1,0:T(8,128)(2,1)S(1)}, u32[]{:S(2)}, u32[]{:S(2)}) collective-permute-start(bf16[9,2,4,16,512]{4,3,2,1,0:T(8,128)(2,1)S(1)} %dynamic-slice_bitcast_fusion.3), channel_id=1, source_target_pairs={{0,1},{1,0},{2,3},{3,2},{4,5},{5,4},{6,7},{7,6},{8,9},{9,8},{10,11... | collective-permute-start | bytes 3538952 | tf_op jit(solution)/shard_map/ppermute | solution.py:328
  394.9 54.7 %collective-permute-start.29 = (bf16[9,2,4,16,512]{4,3,2,1,0:T(8,128)(2,1)S(1)}, bf16[9,2,4,16,512]{4,3,2,1,0:T(8,128)(2,1)S(1)}, u32[]{:S(2)}, u32[]{:S(2)}) collective-permute-start(bf16[9,2,4,16,512]{4,3,2,1,0:T(8,128)(2,1)S(1)} %dynamic-slice_bitcast_fusion.2), channel_id=1, source_target_pairs={{0,1},{1,0},{2,3},{3,2},{4,5},{5,4},{6,7},{7,6},{8,9},{9,8},{10,11... | collective-permute-start | bytes 3538952 | tf_op jit(solution)/shard_map/ppermute | solution.py:328
  407.2 100.2 %collective-permute-start.71 = (bf16[2,2,4,16,512]{4,3,2,1,0:T(8,128)(2,1)S(1)}, bf16[2,2,4,16,512]{4,3,2,1,0:T(8,128)(2,1)S(1)}, u32[]{:S(2)}, u32[]{:S(2)}) collective-permute-start(bf16[2,2,4,16,512]{4,3,2,1,0:T(8,128)(2,1)S(1)} %pad_maximum_fusion.16), channel_id=1, source_target_pairs={{0,2},{2,0},{1,3},{3,1},{4,6},{6,4},{5,7},{7,5},{8,10},{10,8},{9,1... | collective-permute-start | bytes 786440 | tf_op jit(solution)/shard_map/ppermute | solution.py:328
  428.9 22.7 %collective-permute-start.19 = (bf16[9,4,16,512]{3,2,1,0:T(8,128)(2,1)S(1)}, bf16[9,4,16,512]{3,2,1,0:T(8,128)(2,1)S(1)}, u32[]{:S(2)}, u32[]{:S(2)}) collective-permute-start(bf16[9,4,16,512]{3,2,1,0:T(8,128)(2,1)S(1)} %dynamic-slice_bitcast_fusion.9), channel_id=1, source_target_pairs={{0,4},{4,0},{1,5},{5,1},{2,6},{6,2},{3,7},{7,3},{8,12},{12,8},{9,1... | collective-permute-start | bytes 1769480 | tf_op jit(solution)/shard_map/ppermute | solution.py:328
  450.1 11.4 %collective-permute-start.30 = (bf16[9,4,16,512]{3,2,1,0:T(8,128)(2,1)S(1)}, bf16[9,4,16,512]{3,2,1,0:T(8,128)(2,1)S(1)}, u32[]{:S(2)}, u32[]{:S(2)}) collective-permute-start(bf16[9,4,16,512]{3,2,1,0:T(8,128)(2,1)S(1)} %dynamic-slice_bitcast_fusion.8), channel_id=1, source_target_pairs={{0,4},{4,0},{1,5},{5,1},{2,6},{6,2},{3,7},{7,3},{8,12},{12,8},{9,1... | collective-permute-start | bytes 1769480 | tf_op jit(solution)/shard_map/ppermute | solution.py:328
  451.5 75.6 %collective-permute-start.82 = (bf16[2,2,4,16,512]{4,3,2,1,0:T(8,128)(2,1)S(1)}, bf16[2,2,4,16,512]{4,3,2,1,0:T(8,128)(2,1)S(1)}, u32[]{:S(2)}, u32[]{:S(2)}) collective-permute-start(bf16[2,2,4,16,512]{4,3,2,1,0:T(8,128)(2,1)S(1)} %pad_maximum_fusion.17), channel_id=1, source_target_pairs={{0,2},{2,0},{1,3},{3,1},{4,6},{6,4},{5,7},{7,5},{8,10},{10,8},{9,1... | collective-permute-start | bytes 786440 | tf_op jit(solution)/shard_map/ppermute | solution.py:328
  451.9 10.5 %collective-permute-start.20 = (bf16[9,16,512]{2,1,0:T(8,128)(2,1)S(1)}, bf16[9,16,512]{2,1,0:T(8,128)(2,1)S(1)}, u32[]{:S(2)}, u32[]{:S(2)}) collective-permute-start(bf16[9,16,512]{2,1,0:T(8,128)(2,1)S(1)} %get-tuple-element.166), channel_id=1, source_target_pairs={{0,8},{8,16},{16,24},{24,0},{1,9},{9,17},{17,25},{25,1},{2,10},{10... | collective-permute-start | bytes 442376 | tf_op jit(solution)/shard_map/ppermute | solution.py:328
  451.9 15.2 %collective-permute-start.21 = (bf16[9,16,512]{2,1,0:T(8,128)(2,1)S(1)}, bf16[9,16,512]{2,1,0:T(8,128)(2,1)S(1)}, u32[]{:S(2)}, u32[]{:S(2)}) collective-permute-start(bf16[9,16,512]{2,1,0:T(8,128)(2,1)S(1)} %get-tuple-element.168), channel_id=1, source_target_pairs={{0,16},{8,24},{16,0},{24,8},{1,17},{9,25},{17,1},{25,9},{2,18},{10... | collective-permute-start | bytes 442376 | tf_op jit(solution)/shard_map/ppermute | solution.py:328
  461.5 7.9 %collective-permute-start.22 = (bf16[9,16,512]{2,1,0:T(8,128)(2,1)S(1)}, bf16[9,16,512]{2,1,0:T(8,128)(2,1)S(1)}, u32[]{:S(2)}, u32[]{:S(2)}) collective-permute-start(bf16[9,16,512]{2,1,0:T(8,128)(2,1)S(1)} %get-tuple-element.167), channel_id=1, source_target_pairs={{0,24},{8,0},{16,8},{24,16},{1,25},{9,1},{17,9},{25,17},{2,26},{10... | collective-permute-start | bytes 442376 | tf_op jit(solution)/shard_map/ppermute | solution.py:328
  462.4 8.5 %collective-permute-start.31 = (bf16[9,16,512]{2,1,0:T(8,128)(2,1)S(1)}, bf16[9,16,512]{2,1,0:T(8,128)(2,1)S(1)}, u32[]{:S(2)}, u32[]{:S(2)}) collective-permute-start(bf16[9,16,512]{2,1,0:T(8,128)(2,1)S(1)} %get-tuple-element.169), channel_id=1, source_target_pairs={{0,8},{8,16},{16,24},{24,0},{1,9},{9,17},{17,25},{25,1},{2,10},{10... | collective-permute-start | bytes 442376 | tf_op jit(solution)/shard_map/ppermute | solution.py:328
  467.2 12.2 %collective-permute-start.32 = (bf16[9,16,512]{2,1,0:T(8,128)(2,1)S(1)}, bf16[9,16,512]{2,1,0:T(8,128)(2,1)S(1)}, u32[]{:S(2)}, u32[]{:S(2)}) collective-permute-start(bf16[9,16,512]{2,1,0:T(8,128)(2,1)S(1)} %get-tuple-element.171), channel_id=1, source_target_pairs={{0,16},{8,24},{16,0},{24,8},{1,17},{9,25},{17,1},{25,9},{2,18},{10... | collective-permute-start | bytes 442376 | tf_op jit(solution)/shard_map/ppermute | solution.py:328
  469.5 14.9 %collective-permute-start.33 = (bf16[9,16,512]{2,1,0:T(8,128)(2,1)S(1)}, bf16[9,16,512]{2,1,0:T(8,128)(2,1)S(1)}, u32[]{:S(2)}, u32[]{:S(2)}) collective-permute-start(bf16[9,16,512]{2,1,0:T(8,128)(2,1)S(1)} %get-tuple-element.170), channel_id=1, source_target_pairs={{0,24},{8,0},{16,8},{24,16},{1,25},{9,1},{17,9},{25,17},{2,26},{10... | collective-permute-start | bytes 442376 | tf_op jit(solution)/shard_map/ppermute | solution.py:328
  470.9 13.7 %collective-permute-start.23 = (bf16[9,16,512]{2,1,0:T(8,128)(2,1)S(1)}, bf16[9,16,512]{2,1,0:T(8,128)(2,1)S(1)}, u32[]{:S(2)}, u32[]{:S(2)}) collective-permute-start(bf16[9,16,512]{2,1,0:T(8,128)(2,1)S(1)} %get-tuple-element.127), channel_id=1, source_target_pairs={{0,8},{8,16},{16,24},{24,0},{1,9},{9,17},{17,25},{25,1},{2,10},{10... | collective-permute-start | bytes 442376 | tf_op jit(solution)/shard_map/ppermute | solution.py:328
  479.4 12.7 %collective-permute-start.24 = (bf16[9,16,512]{2,1,0:T(8,128)(2,1)S(1)}, bf16[9,16,512]{2,1,0:T(8,128)(2,1)S(1)}, u32[]{:S(2)}, u32[]{:S(2)}) collective-permute-start(bf16[9,16,512]{2,1,0:T(8,128)(2,1)S(1)} %get-tuple-element.127), channel_id=1, source_target_pairs={{0,16},{8,24},{16,0},{24,8},{1,17},{9,25},{17,1},{25,9},{2,18},{10... | collective-permute-start | bytes 442376 | tf_op jit(solution)/shard_map/ppermute | solution.py:328
  484.4 12.7 %collective-permute-start.25 = (bf16[9,16,512]{2,1,0:T(8,128)(2,1)S(1)}, bf16[9,16,512]{2,1,0:T(8,128)(2,1)S(1)}, u32[]{:S(2)}, u32[]{:S(2)}) collective-permute-start(bf16[9,16,512]{2,1,0:T(8,128)(2,1)S(1)} %get-tuple-element.127), channel_id=1, source_target_pairs={{0,24},{8,0},{16,8},{24,16},{1,25},{9,1},{17,9},{25,17},{2,26},{10... | collective-permute-start | bytes 442376 | tf_op jit(solution)/shard_map/ppermute | solution.py:328
  484.6 12.5 %collective-permute-start.34 = (bf16[9,16,512]{2,1,0:T(8,128)(2,1)S(1)}, bf16[9,16,512]{2,1,0:T(8,128)(2,1)S(1)}, u32[]{:S(2)}, u32[]{:S(2)}) collective-permute-start(bf16[9,16,512]{2,1,0:T(8,128)(2,1)S(1)} %get-tuple-element.129), channel_id=1, source_target_pairs={{0,8},{8,16},{16,24},{24,0},{1,9},{9,17},{17,25},{25,1},{2,10},{10... | collective-permute-start | bytes 442376 | tf_op jit(solution)/shard_map/ppermute | solution.py:328
  492.0 11.8 %collective-permute-start.35 = (bf16[9,16,512]{2,1,0:T(8,128)(2,1)S(1)}, bf16[9,16,512]{2,1,0:T(8,128)(2,1)S(1)}, u32[]{:S(2)}, u32[]{:S(2)}) collective-permute-start(bf16[9,16,512]{2,1,0:T(8,128)(2,1)S(1)} %get-tuple-element.129), channel_id=1, source_target_pairs={{0,16},{8,24},{16,0},{24,8},{1,17},{9,25},{17,1},{25,9},{2,18},{10... | collective-permute-start | bytes 442376 | tf_op jit(solution)/shard_map/ppermute | solution.py:328
  497.1 9.5 %collective-permute-start.36 = (bf16[9,16,512]{2,1,0:T(8,128)(2,1)S(1)}, bf16[9,16,512]{2,1,0:T(8,128)(2,1)S(1)}, u32[]{:S(2)}, u32[]{:S(2)}) collective-permute-start(bf16[9,16,512]{2,1,0:T(8,128)(2,1)S(1)} %get-tuple-element.129), channel_id=1, source_target_pairs={{0,24},{8,0},{16,8},{24,16},{1,25},{9,1},{17,9},{25,17},{2,26},{10... | collective-permute-start | bytes 442376 | tf_op jit(solution)/shard_map/ppermute | solution.py:328
  497.1 16.3 %collective-permute-start.26 = (bf16[9,4,16,512]{3,2,1,0:T(8,128)(2,1)S(1)}, bf16[9,4,16,512]{3,2,1,0:T(8,128)(2,1)S(1)}, u32[]{:S(2)}, u32[]{:S(2)}) collective-permute-start(bf16[9,4,16,512]{3,2,1,0:T(8,128)(2,1)S(1)} %bitcast_dynamic-update-slice_fusion.12), channel_id=1, source_target_pairs={{0,4},{4,0},{1,5},{5,1},{2,6},{6,2},{3,7},{7,3},{8,12},{12,8},{9,1... | collective-permute-start | bytes 1769480 | tf_op jit(solution)/shard_map/ppermute | solution.py:328
  506.6 18.5 %collective-permute-start.37 = (bf16[9,4,16,512]{3,2,1,0:T(8,128)(2,1)S(1)}, bf16[9,4,16,512]{3,2,1,0:T(8,128)(2,1)S(1)}, u32[]{:S(2)}, u32[]{:S(2)}) collective-permute-start(bf16[9,4,16,512]{3,2,1,0:T(8,128)(2,1)S(1)} %bitcast_dynamic-update-slice_fusion.8), channel_id=1, source_target_pairs={{0,4},{4,0},{1,5},{5,1},{2,6},{6,2},{3,7},{7,3},{8,12},{12,8},{9,1... | collective-permute-start | bytes 1769480 | tf_op jit(solution)/shard_map/ppermute | solution.py:328
  514.6 16.8 %collective-permute-start.27 = (bf16[9,2,4,16,512]{4,3,2,1,0:T(8,128)(2,1)}, bf16[9,2,4,16,512]{4,3,2,1,0:T(8,128)(2,1)}, u32[]{:S(2)}, u32[]{:S(2)}) collective-permute-start(bf16[9,2,4,16,512]{4,3,2,1,0:T(8,128)(2,1)} %pad_maximum_fusion.12), channel_id=1, source_target_pairs={{0,2},{2,0},{1,3},{3,1},{4,6},{6,4},{5,7},{7,5},{8,10},{10,8},{9,1... | collective-permute-start | bytes 3538952 | tf_op jit(solution)/shard_map/ppermute | solution.py:328
  (65 other events, 580.6 us)
